TPU v7x, 256 devices: a whole 4x4x8 slice. The times are simulated.
256 devices in a mesh: dp: 32 (over x, y, z_hi), tensor: 8 (over z_lo, core).
Axes of the slice: x: 4, y: 4, z: 8 (z_hi: 2, z_lo: 4; z = z_hi * 4 + z_lo), core: 2. Of those that a mesh axis runs over, the one named last changes fastest.
Arguments:
- hidden: bfloat16 [32768, 8192], P(('dp', 'tensor')), may hold values from -24 to 24
- w_key: bfloat16 [8192, 1024], P(None, 'tensor'), may hold values from -0.0625 to 0.0625
- value_weight: bfloat16 [8192, 1024], P(None, 'tensor'), may hold values from -0.0625 to 0.0625
- value_down_factor: bfloat16 [32, 8192], replicated, may hold values from -0.0625 to 0.0625
- value_up_factor: bfloat16 [32, 1024], P(None, 'tensor'), may hold values from -0.5 to 0.5
- mag_value: float32 [1024], P('tensor'), may hold values from 0.5 to 2
- queries: bfloat16 [32768, 4096], P('dp', 'tensor'), may hold values from -1200 to 1200
- grad_attn: bfloat16 [32768, 4096], P('dp', 'tensor'), may hold values from -6 to 6
Outputs:
- grad_hidden: bfloat16 [32768, 8192], P(('dp', 'tensor'))
- grad_down: float32 [32, 8192], P(None, ('dp', 'tensor'))
- grad_up: float32 [32, 1024], P(None, 'tensor')
- grad_mag: float32 [1024], P('tensor')
All inputs are finite; a program needn't handle non-finite values.
Results may differ from a plain program's by a relative error of at most 0.04.
Values may be sent and summed in bfloat16 or wider, within the bound.
No kernel may reach another device: no remote copies, remote signals or barrier semaphores. Data moves between devices by JAX's collectives and lax.ppermute only.
A program may use at most 192 MiB of HBM per device.

v0:
```python
import jax
import jax.numpy as jnp
import numpy as np
from jax import lax
from jax.experimental import pallas as pl
from jax.experimental.pallas import tpu as pltpu
from jax.sharding import Mesh, PartitionSpec as P

HD = 128
D = 8192
SEQ = 1024
RANK = 32
PAIR = 256
NEAR = 5120
LINE = 3072
CHUNK = 1280
QB = 256
GROUP = 4
SCALE = 2.0
ROPE_BASE = 500000.0
LOG2E = 1.4426950408889634
INV_SQRT = HD ** (-0.5)
MIB = 1024 * 1024
BF = jnp.bfloat16
F32 = jnp.float32
NT = (((1,), (1,)), ((), ()))
TN = (((0,), (0,)), ((), ()))
EVERY = ("x", "y", "zh", "zl", "core")
DP = ("x", "y", "zh")


def rope_tables():
    half = HD // 2
    frequency = ROPE_BASE ** (-(jnp.arange(half, dtype=F32) * 2.0 / HD))
    angles = jnp.arange(SEQ, dtype=F32)[:, None] * frequency[None, :]
    cosine, sine = jnp.cos(angles), jnp.sin(angles)
    return jnp.concatenate([cosine, cosine], 1), jnp.concatenate([-sine, sine], 1)


def smem():
    return pl.BlockSpec(memory_space=pltpu.SMEM)


def whole(shape):
    return pl.BlockSpec(shape, lambda *_: (0,) * len(shape))


def params(limit):
    return pltpu.CompilerParams(vmem_limit_bytes=limit * MIB)


def cost(flops, moved, trans=0):
    return pl.CostEstimate(flops=flops, bytes_accessed=moved, transcendentals=trans)


def any_ref():
    return pl.BlockSpec(memory_space=pl.ANY)


def start_all(copies):
    for copy in copies:
        copy.start()
    return copies


def wait_all(copies):
    for copy in copies:
        copy.wait()


def near_copies(base, first, own_key, own_val, far, weights, sems):
    chunks = []
    for i in range(far.shape[0] // CHUNK):
        here = pl.ds(first + i * CHUNK, CHUNK)
        near = pl.ds(i * CHUNK, CHUNK)
        there = pl.ds(base + i * CHUNK, CHUNK)
        chunks.append(
            [
                pltpu.make_async_copy(own_key.at[there, :], weights.at[here, pl.ds(0, HD)], sems.at[0, i]),
                pltpu.make_async_copy(own_val.at[there, :], weights.at[here, pl.ds(HD, HD)], sems.at[1, i]),
                pltpu.make_async_copy(far.at[near, :], weights.at[here, pl.ds(256, 768)], sems.at[2, i]),
            ]
        )
    return chunks


def line_copies(base, first, own_key, own_val, one, two_a, two_b, three, weights, sems):
    chunks = []
    size = LINE // 2
    for i, two in enumerate((two_a.at[pl.ds(RANK, size), :], two_b)):
        here = pl.ds(first + i * size, size)
        there = pl.ds(base + i * size, size)
        near = pl.ds(RANK + i * size, size)
        chunks.append(
            [
                pltpu.make_async_copy(own_key.at[there, :], weights.at[here, pl.ds(0, HD)], sems.at[0, i]),
                pltpu.make_async_copy(own_val.at[there, :], weights.at[here, pl.ds(HD, HD)], sems.at[1, i]),
                pltpu.make_async_copy(one.at[near, :], weights.at[here, pl.ds(256, 256)], sems.at[2, i]),
                pltpu.make_async_copy(two, weights.at[here, pl.ds(512, 256)], sems.at[3, i]),
                pltpu.make_async_copy(three.at[near, :], weights.at[here, pl.ds(768, 256)], sems.at[4, i]),
            ]
        )
    return chunks


def pair_copies(pair, hid, base, count, sem):
    size = hid.shape[1] // count
    return [
        pltpu.make_async_copy(
            pair.at[:, pl.ds(base + i * size, size)], hid.at[:, pl.ds(i * size, size)], sem.at[i]
        )
        for i in range(count)
    ]


def multiply(acc, chunks, hid_chunks, hid, weights):
    size = hid.shape[1] // len(chunks)
    for i, chunk in enumerate(chunks):
        wait_all(chunk + [hid_chunks[i]])
        here = slice(i * size, (i + 1) * size)
        term = jnp.dot(hid[:, here], weights[here, :], preferred_element_type=F32)
        acc = term if acc is None else acc + term
    return acc


def project_line_kernel(
    pair, own_key, own_val, one, two_a, two_b, three, out, hid, weights, hid_sem, sems
):
    chunks = line_copies(NEAR, 0, own_key, own_val, one, two_a, two_b, three, weights, sems)
    hid_chunks = pair_copies(pair, hid, NEAR, 2, hid_sem)
    for i in range(2):
        start_all(chunks[i] + [hid_chunks[i]])
    out[...] = multiply(None, chunks, hid_chunks, hid, weights)


def project_line(pair, w_key, w_val, line):
    return pl.pallas_call(
        project_line_kernel,
        in_specs=[any_ref()] * 7,
        out_specs=whole((PAIR, 1024)),
        out_shape=jax.ShapeDtypeStruct((PAIR, 1024), F32),
        scratch_shapes=[
            pltpu.VMEM((PAIR, LINE), BF),
            pltpu.VMEM((LINE, 1024), BF),
            pltpu.SemaphoreType.DMA((2,)),
            pltpu.SemaphoreType.DMA((5, 2)),
        ],
        compiler_params=params(60),
        cost_estimate=cost(2 * PAIR * LINE * 1024, 8 * MIB),
        name="project_line",
    )(pair, w_key, w_val, *line)


def project_kernel(
    place, pair, own_key, own_val, far, so_far, down, ups, cos, sin, out, hid, weights, hid_sem, sems
):
    count = NEAR // CHUNK
    chunks = near_copies(0, 0, own_key, own_val, far, weights, sems)
    hid_chunks = pair_copies(pair, hid, 0, count, hid_sem)
    for i in range(count):
        start_all(chunks[i] + [hid_chunks[i]])
    acc = multiply(so_far[...], chunks, hid_chunks, hid, weights)
    packed = jnp.concatenate([down[64 * j : 64 * j + 64, :] for j in range(4)], axis=1)
    packed = jnp.concatenate([packed[:32], packed[32:], jnp.zeros((32, HD), BF)], axis=1)
    for r in range(4):
        key = acc[:, r * 256 : r * 256 + HD]
        turned = key * cos[...] + pltpu.roll(key, HD // 2, 1) * sin[...]
        turned = turned * (INV_SQRT * LOG2E)
        high = turned.astype(BF)
        low = (turned - high.astype(F32)).astype(BF)
        lifted = jnp.dot(down[...], ups[r], preferred_element_type=F32)
        base = (acc[:, r * 256 + HD : (r + 1) * 256] + SCALE * lifted).astype(BF)
        slot = lax.rem(place[0] + r, 4)
        out[slot, :PAIR, :] = jnp.concatenate([high, low, base], axis=1)
        out[slot, PAIR:, :] = packed


def project(place, pair, w_key, w_val, far, so_far, down, ups, cos, sin):
    count = NEAR // CHUNK
    return pl.pallas_call(
        project_kernel,
        in_specs=[
            smem(),
            any_ref(),
            any_ref(),
            any_ref(),
            any_ref(),
            whole((PAIR, 1024)),
            whole((PAIR, RANK)),
            whole((4, RANK, HD)),
            whole((PAIR, HD)),
            whole((PAIR, HD)),
        ],
        out_specs=whole((4, PAIR + 32, 3 * HD)),
        out_shape=jax.ShapeDtypeStruct((4, PAIR + 32, 3 * HD), BF),
        scratch_shapes=[
            pltpu.VMEM((PAIR, NEAR), BF),
            pltpu.VMEM((NEAR, 1024), BF),
            pltpu.SemaphoreType.DMA((count,)),
            pltpu.SemaphoreType.DMA((3, count)),
        ],
        compiler_params=params(60),
        cost_estimate=cost(2 * PAIR * NEAR * 1024, 14 * MIB),
        name="project",
    )(place, pair, w_key, w_val, far, so_far, down, ups, cos, sin)


def attend_kernel(query, grad, rows, col_scale, cos, sin, grads, up_grad, mag_grad, keys, vals, dkey, dval):
    head = pl.program_id(0)

    @pl.when(head == 0)
    def _():
        for i in range(4):
            here = slice(i * PAIR, (i + 1) * PAIR)
            keys[here, :] = rows[i, :PAIR, : 2 * HD]
            vals[here, :] = (rows[i, :PAIR, 2 * HD :].astype(F32) * col_scale[...]).astype(BF)
        dkey[...] = jnp.zeros_like(dkey)
        dval[...] = jnp.zeros_like(dval)

    for block in range(SEQ // QB):
        stop = (block + 1) * QB
        here = slice(block * QB, stop)
        q = query[here, :]
        g = grad[here, :]
        qq = jnp.concatenate([q, q], axis=1)
        scores = lax.dot_general(keys[:stop], qq, NT, preferred_element_type=F32)
        key_at = lax.broadcasted_iota(jnp.int32, (QB, QB), 0)
        query_at = lax.broadcasted_iota(jnp.int32, (QB, QB), 1)
        edge = jnp.where(key_at <= query_at, scores[block * QB :], -1e30)
        if block:
            scores = jnp.concatenate([scores[: block * QB], edge], axis=0)
        else:
            scores = edge
        powers = jnp.exp2(scores - jnp.max(scores, axis=0, keepdims=True))
        attn = powers * (1.0 / jnp.sum(powers, axis=0, keepdims=True))
        half = attn.astype(BF)
        pgrad = lax.dot_general(vals[:stop], g, NT, preferred_element_type=F32)
        delta = jnp.sum(half.astype(F32) * pgrad, axis=0, keepdims=True)
        sgrad = (attn * (pgrad - delta)).astype(BF)
        dval[:stop] += jnp.dot(half, g, preferred_element_type=F32)
        dkey[:stop] += jnp.dot(sgrad, q, preferred_element_type=F32)

    @pl.when(head == pl.num_programs(0) - 1)
    def _():
        dk = dkey[...] * INV_SQRT
        dk = dk * cos[...] - pltpu.roll(dk, HD // 2, 1) * sin[...]
        dv = dval[...]
        gv = (dv * col_scale[...]).astype(BF)
        grads[:, :HD] = dk.astype(BF)
        grads[:, HD:] = gv
        total = jnp.zeros((RANK, HD), F32)
        mags = jnp.zeros((1, HD), F32)
        for i in range(4):
            here = slice(i * PAIR, (i + 1) * PAIR)
            packed = rows[i, PAIR:, : 2 * HD]
            packed = jnp.concatenate([packed[:, :HD], packed[:, HD:]], axis=0)
            down = jnp.concatenate([packed[:, 32 * j : 32 * j + 32] for j in range(4)], axis=0)
            total += lax.dot_general(down, gv[here], TN, preferred_element_type=F32)
            mags += jnp.sum(dv[here] * rows[i, :PAIR, 2 * HD :].astype(F32), axis=0, keepdims=True)
        up_grad[...] = SCALE * total
        mag_grad[...] = jnp.broadcast_to(mags, mag_grad.shape)


def attend(queries, grad_attn, rows, col_scale, cos, sin):
    return pl.pallas_call(
        attend_kernel,
        grid=(GROUP,),
        in_specs=[
            pl.BlockSpec((SEQ, HD), lambda h: (0, h)),
            pl.BlockSpec((SEQ, HD), lambda h: (0, h)),
            whole((4, PAIR + 32, 3 * HD)),
            whole((1, HD)),
            whole((SEQ, HD)),
            whole((SEQ, HD)),
        ],
        out_specs=[whole((SEQ, 2 * HD)), whole((RANK, HD)), whole((8, HD))],
        out_shape=[
            jax.ShapeDtypeStruct((SEQ, 2 * HD), BF),
            jax.ShapeDtypeStruct((RANK, HD), F32),
            jax.ShapeDtypeStruct((8, HD), F32),
        ],
        scratch_shapes=[
            pltpu.VMEM((SEQ, 2 * HD), BF),
            pltpu.VMEM((SEQ, HD), BF),
            pltpu.VMEM((SEQ, HD), F32),
            pltpu.VMEM((SEQ, HD), F32),
        ],
        compiler_params=params(60),
        cost_estimate=cost(5 * 2 * GROUP * SEQ * SEQ * HD, 6 * MIB, GROUP * SEQ * SEQ),
        name="attend",
    )(queries, grad_attn, rows, col_scale, cos, sin)


def rank_kernel(place, grads, ups, out):
    total = jnp.zeros((PAIR, RANK), F32)
    for r in range(4):
        slot = lax.rem(place[0] + r, 4)
        total += lax.dot_general(grads[slot, :, HD:], ups[r], NT, preferred_element_type=F32)
    out[...] = total


def rank_part(place, grads, ups):
    return pl.pallas_call(
        rank_kernel,
        in_specs=[smem(), whole((4, PAIR, 2 * HD)), whole((4, RANK, HD))],
        out_specs=whole((PAIR, RANK)),
        out_shape=jax.ShapeDtypeStruct((PAIR, RANK), F32),
        compiler_params=params(60),
        cost_estimate=cost(2 * PAIR * 512 * RANK, MIB),
        name="rank_part",
    )(place, grads, ups)


def back_kernel(
    place, grads, own_key, own_val, far, one, two_a, two_b, three, _, mine, theirs,
    left, weights, part, far_sems, line_sems, out_sem,
):
    chunks = near_copies(0, 0, own_key, own_val, far, weights, far_sems)
    chunks += line_copies(NEAR, NEAR, own_key, own_val, one, two_a, two_b, three, weights, line_sems)
    for chunk in chunks:
        start_all(chunk)
    first = pl.multiple_of(place[1] * 128, 128)
    second = pl.multiple_of(128 - place[1] * 128, 128)
    for r in range(4):
        slot = lax.rem(place[0] + r, 4)
        left[:128, r * 256 : (r + 1) * 256] = grads[slot, pl.ds(first, 128), :]
        left[128:, r * 256 : (r + 1) * 256] = grads[slot, pl.ds(second, 128), :]
    leaving = []
    base = 0
    for i, chunk in enumerate(chunks):
        size = CHUNK if i < NEAR // CHUNK else LINE // 2
        wait_all(chunk)
        here = slice(base, base + size)
        part[:, here] = lax.dot_general(left[...], weights[here, :], NT, preferred_element_type=F32).astype(BF)
        cols = pl.ds(base, size)
        leaving += start_all(
            [
                pltpu.make_async_copy(part.at[pl.ds(128, 128), cols], theirs.at[:, cols], out_sem.at[0, i]),
                pltpu.make_async_copy(part.at[pl.ds(0, 128), cols], mine.at[:, cols], out_sem.at[1, i]),
            ]
        )
        base += size
    wait_all(leaving)


def back(place, grads, w_key, w_val, far, line, after):
    count = NEAR // CHUNK
    return pl.pallas_call(
        back_kernel,
        in_specs=[smem(), whole((4, PAIR, 2 * HD))] + [any_ref()] * 8,
        out_specs=[any_ref()] * 2,
        out_shape=[jax.ShapeDtypeStruct((128, D), BF)] * 2,
        scratch_shapes=[
            pltpu.VMEM((PAIR, 1024), BF),
            pltpu.VMEM((D, 1024), BF),
            pltpu.VMEM((PAIR, D), BF),
            pltpu.SemaphoreType.DMA((3, count)),
            pltpu.SemaphoreType.DMA((5, 2)),
            pltpu.SemaphoreType.DMA((2, count + 2)),
        ],
        compiler_params=params(60),
        cost_estimate=cost(2 * PAIR * D * 1024, 20 * MIB),
        name="back",
    )(place, grads, w_key, w_val, far, *line, after)


def join_kernel(place, rank, factor, mine, theirs, out, one, two, result, sems, out_sem):
    size = D // 8
    chunks = []
    for i in range(8):
        cols = pl.ds(i * size, size)
        chunks.append(
            start_all(
                [
                    pltpu.make_async_copy(mine.at[:, cols], one.at[:, cols], sems.at[0, i]),
                    pltpu.make_async_copy(theirs.at[:, cols], two.at[:, cols], sems.at[1, i]),
                ]
            )
        )
    own = rank[pl.ds(pl.multiple_of(place[1] * 128, 128), 128), :]
    leaving = []
    for i, chunk in enumerate(chunks):
        here = slice(i * size, (i + 1) * size)
        adapter = SCALE * jnp.dot(own, factor[:, here], preferred_element_type=F32)
        wait_all(chunk)
        result[:, here] = (one[:, here].astype(F32) + two[:, here].astype(F32) + adapter).astype(BF)
        cols = pl.ds(i * size, size)
        leaving += start_all([pltpu.make_async_copy(result.at[:, cols], out.at[:, cols], out_sem.at[i])])
    wait_all(leaving)


def join(place, rank, factor, mine, theirs):
    return pl.pallas_call(
        join_kernel,
        in_specs=[smem(), whole((PAIR, RANK)), whole((RANK, D)), any_ref(), any_ref()],
        out_specs=any_ref(),
        out_shape=jax.ShapeDtypeStruct((128, D), BF),
        scratch_shapes=[pltpu.VMEM((128, D), BF)] * 3
        + [pltpu.SemaphoreType.DMA((2, 8)), pltpu.SemaphoreType.DMA((8,))],
        compiler_params=params(60),
        cost_estimate=cost(0, 0),
        name="join",
    )(place, rank, factor, mine, theirs)


def down_kernel(place, rank, hid, out):
    part = SCALE * lax.dot_general(rank[...], hid[...], TN, preferred_element_type=F32)
    lane = lax.broadcasted_iota(jnp.int32, (8, HD), 1) // 32
    core = place[1]
    for tile in range(part.shape[1] // HD):
        regs = [part[8 * i : 8 * i + 8, tile * HD : (tile + 1) * HD] for i in range(4)]
        blocks = []
        for pick in range(2):
            column = 2 * pick + core
            block = jnp.zeros((8, HD), F32)
            for i in range(4):
                moved = pltpu.roll(regs[i], lax.rem((i - column + 4) * 32, HD), 1)
                block = jnp.where(lane == i, moved, block)
            blocks.append(block)
        out[16 * tile : 16 * tile + 16, :] = jnp.concatenate(blocks, axis=0).astype(BF)


def down_part(place, rank, pair):
    wide = 2048
    return pl.pallas_call(
        down_kernel,
        grid=(D // wide,),
        in_specs=[smem(), whole((PAIR, RANK)), pl.BlockSpec((PAIR, wide), lambda k: (0, k))],
        out_specs=pl.BlockSpec((wide // 8, HD), lambda k: (k, 0)),
        out_shape=jax.ShapeDtypeStruct((1024, HD), BF),
        compiler_params=params(60),
        cost_estimate=cost(2 * PAIR * D * RANK, 5 * MIB),
        name="down_part",
    )(place, rank, pair)


def finish_kernel(pieces, small, _, out, up_grad, mag_grad):
    total = jnp.sum(pieces[...].astype(F32).reshape(128, 8, HD), axis=0)
    for i in range(4):
        out[8 * i : 8 * i + 8, :] = total[:, 32 * i : 32 * i + 32]
    sums = jnp.sum(small[...], axis=0)
    up_grad[...] = sums[:RANK]
    mag_grad[...] = sums[RANK:]


def finish(pieces, small, after):
    return pl.pallas_call(
        finish_kernel,
        grid=(1,),
        in_specs=[whole((1024, HD)), whole((16, 40, HD)), any_ref()],
        out_specs=[whole((RANK, 32)), whole((RANK, HD)), whole((8, HD))],
        out_shape=[
            jax.ShapeDtypeStruct((RANK, 32), F32),
            jax.ShapeDtypeStruct((RANK, HD), F32),
            jax.ShapeDtypeStruct((8, HD), F32),
        ],
        compiler_params=params(60),
        cost_estimate=cost(0, 0),
        name="finish",
    )(pieces, small, after)


def along_z(value, shift):
    return lax.ppermute(value, ("zh", "zl"), [(i, (i + shift) % 8) for i in range(8)])


def gather_weights(w_key, w_val, up):
    count = NEAR // 16
    at = (lax.axis_index("x") * 4 + lax.axis_index("y")) * count
    seed = jnp.concatenate([lax.dynamic_slice(w, (at, 0), (count, HD)) for w in (w_key, w_val)], axis=1)
    half = count // 2
    first = along_z(seed, -1)
    third = along_z(seed, 1)
    second = jnp.concatenate([along_z(seed[:half], -2), along_z(seed[half:], 2)], axis=0)
    far = lax.all_gather(jnp.concatenate([first, second, third], axis=1), ("x", "y"), axis=0, tiled=True)
    own = jnp.concatenate([w_key[NEAR:], w_val[NEAR:]], axis=1)
    own = jnp.concatenate([jnp.pad(up, ((0, 0), (0, HD))), own], axis=0) + seed[:1, :1] * 0
    one = along_z(own, -1)
    three = along_z(own, 1)
    two_a = along_z(one[: RANK + LINE // 2], -1)
    two_b = along_z(three[RANK + LINE // 2 :], 1)
    ups = jnp.stack([up] + [got[:RANK, :HD] for got in (one, two_a, three)])
    return far, (one, two_a, two_b, three), ups


def shards(hidden, w_key, w_val, factor, up, mag, queries, grad_attn):
    zl, core = lax.axis_index("zl"), lax.axis_index("core")
    place = jnp.stack([zl, core]).astype(jnp.int32)
    swap = [(0, 1), (1, 0)]
    other = lax.ppermute(hidden, "core", swap)
    pair = jnp.where(
        core == 0, jnp.concatenate([hidden, other], axis=0), jnp.concatenate([other, hidden], axis=0)
    )
    down = lax.dot_general(pair, factor, NT, preferred_element_type=F32).astype(BF)
    far, line, ups = gather_weights(w_key, w_val, up)
    merged = w_val.astype(F32) + SCALE * lax.dot_general(factor, up, TN, preferred_element_type=F32)
    norms = jnp.sqrt(jnp.sum(merged * merged, axis=0))
    col_scale = (mag / norms).reshape(1, HD)
    cos, sin = rope_tables()
    cos_here = lax.dynamic_slice(cos, (zl * PAIR, 0), (PAIR, HD))
    sin_here = lax.dynamic_slice(sin, (zl * PAIR, 0), (PAIR, HD))
    so_far = project_line(pair, w_key, w_val, line)
    rows = project(place, pair, w_key, w_val, far, so_far, down, ups, cos_here, sin_here)
    rows = lax.all_to_all(rows, "zl", 0, 0, tiled=True)
    grads, up_grad, mag_grad = attend(queries, grad_attn, rows, col_scale, cos, sin)
    grads = lax.all_to_all(grads.reshape(4, PAIR, 2 * HD), "zl", 0, 0, tiled=True)
    small = jnp.concatenate([up_grad, mag_grad / norms], axis=0)
    small = small + lax.ppermute(small, "zh", swap)
    padded = jnp.pad(small, ((0, 88), (0, 0)))
    small = lax.all_gather(padded, ("x", "y"), axis=0, tiled=True)
    part = rank_part(place, grads, ups)
    rank = (part + lax.ppermute(part, "core", swap)).astype(BF)
    mine, theirs = back(place, grads, w_key, w_val, far, line, padded)
    theirs = lax.ppermute(theirs, "core", swap)
    pieces = lax.all_to_all(down_part(place, rank, pair), DP + ("zl",), 0, 0, tiled=True)
    grad_hidden = join(place, rank, factor, mine, theirs)
    grad_down, up_sum, mag_sum = finish(pieces, small.reshape(16, HD, HD), grad_hidden)
    return grad_hidden, grad_down, up_sum, mag_sum[0]


def solution(mesh):
    fine = Mesh(np.asarray(mesh.devices).reshape(4, 4, 2, 4, 2), EVERY)
    tensor = ("zl", "core")
    return jax.shard_map(
        shards,
        mesh=fine,
        in_specs=(
            P(EVERY, None),
            P(None, tensor),
            P(None, tensor),
            P(),
            P(None, tensor),
            P(tensor),
            P(DP, tensor),
            P(DP, tensor),
        ),
        out_specs=(P(EVERY, None), P(None, EVERY), P(None, tensor), P(tensor)),
        check_vma=False,
    )
```

profile of v0, /device:TPU:1, one launch (start us, length us, event | category | flops | bytes accessed | tf_op | source)
XLA Modules:
  0.0 233.6 jit_solution(5056423587200200770)
XLA Ops:
  7.2 0.0 slice-start
  7.2 0.0 all-gather.3.cloned.1.call-start
  7.3 1.0 constant_dynamic-slice_fusion.1
  8.3 2.5 %collective-permute-start.4 = (bf16[320,256]{1,0:T(8,128)(2,1)S(1)}, bf16[320,256]{1,0:T(8,128)(2,1)S(1)}, u32[]{:S(2)}, u32[]{:S(2)}) collective-permute-start(bf16[320,256]{1,0:T(8,128)(2,1)S(1)} %pad_maximum_fusion.3), channel_id=1, source_target_pairs={{0,2},{2,4},{4,6},{6,8},{8,10},{10,12},{12,14},{14,0},{1,3},{3,5},... | collective-permute-start | bytes 491528 | tf_op jit(solution)/shard_map/ppermute | solution.py:464
  10.9 4.0 %collective-permute-start.1 = (bf16[320,256]{1,0:T(8,128)(2,1)S(1)}, bf16[320,256]{1,0:T(8,128)(2,1)S(1)}, u32[]{:S(2)}, u32[]{:S(2)}) collective-permute-start(bf16[320,256]{1,0:T(8,128)(2,1)S(1)} %pad_maximum_fusion.3), channel_id=1, source_target_pairs={{0,14},{2,0},{4,2},{6,4},{8,6},{10,8},{12,10},{14,12},{1,15},{3,1}... | collective-permute-start | bytes 491528 | tf_op jit(solution)/shard_map/ppermute | solution.py:464
  14.9 1.9 collective-permute-start.2
  16.8 0.5 collective-permute-start.3
  17.4 3.2 %collective-permute-done.2 = bf16[160,256]{1,0:T(8,128)(2,1)S(1)} collective-permute-done((bf16[160,256]{1,0:T(8,128)(2,1)S(1)}, bf16[160,256]{1,0:T(8,128)(2,1)S(1)}, u32[]{:S(2)}, u32[]{:S(2)}) %collective-permute-start.2) | collective-permute-done | bytes 81952 | tf_op jit(solution)/shard_map/ppermute | solution.py:464
  20.6 2.1 collective-permute-done.3
  22.7 0.8 pad_maximum_fusion.2
  23.5 0.0 all-gather.3.cloned.1.call-update
  23.5 3.0 %collective-permute-start = (bf16[128,8192]{1,0:T(8,128)(2,1)}, bf16[128,8192]{1,0:T(8,128)(2,1)}, u32[]{:S(2)}, u32[]{:S(2)}) collective-permute-start(bf16[128,8192]{1,0:T(8,128)(2,1)} %param.8), channel_id=1, source_target_pairs={{0,1},{1,0},{2,3},{3,2},{4,5},{5,4},{6,7},{7,6},{8,9},{9,8},{10,11... | collective-permute-start | bytes 6291464 | tf_op jit(solution)/shard_map/ppermute | solution.py:490
  26.5 1.2 fusion.15
  27.7 2.1 fusion.5
  29.8 0.1 collective-permute-start.7
  29.9 2.6 %collective-permute-start.5 = (bf16[3104,256]{1,0:T(8,128)(2,1)}, bf16[3104,256]{1,0:T(8,128)(2,1)S(1)}, u32[]{:S(2)}, u32[]{:S(2)}) collective-permute-start(bf16[3104,256]{1,0:T(8,128)(2,1)} %fusion.5), channel_id=1, source_target_pairs={{0,14},{2,0},{4,2},{6,4},{8,6},{10,8},{12,10},{14,12},{1,15},{3,1}... | collective-permute-start | bytes 4767752 | tf_op jit(solution)/shard_map/ppermute | solution.py:464
  32.4 0.7 pad_add_fusion.place
  33.1 2.0 fusion.6
  35.1 0.8 copy-done.5
  35.8 0.8 fusion.9
  36.7 30.9 %collective-permute-done.7.three = bf16[3104,256]{1,0:T(8,128)(2,1)S(1)} collective-permute-done((bf16[3104,256]{1,0:T(8,128)(2,1)}, bf16[3104,256]{1,0:T(8,128)(2,1)S(1)}, u32[]{:S(2)}, u32[]{:S(2)}) %collective-permute-start.7) | collective-permute-done | bytes 1589280 | tf_op jit(solution)/shard_map/ppermute | solution.py:464
  67.6 1.1 slice.49
  68.7 1.0 slice.48
  69.7 2.7 %collective-permute-start.6 = (bf16[1568,256]{1,0:T(8,128)(2,1)}, bf16[1568,256]{1,0:T(8,128)(2,1)}, u32[]{:S(2)}, u32[]{:S(2)}) collective-permute-start(bf16[1568,256]{1,0:T(8,128)(2,1)} %slice.48), channel_id=1, source_target_pairs={{0,14},{2,0},{4,2},{6,4},{8,6},{10,8},{12,10},{14,12},{1,15},{3,1}... | collective-permute-start | bytes 2408456 | tf_op jit(solution)/shard_map/ppermute | solution.py:464
  72.4 3.2 %maximum_select_fusion.pair.hid = bf16[256,8192]{1,0:T(8,128)(2,1)S(1)} fusion(bf16[128,8192]{1,0:T(8,128)(2,1)} %collective-permute-done, bf16[128,8192]{1,0:T(8,128)(2,1)S(1)} %copy-done.11, pred[]{:T(512)S(6)} %eq.3), kind=kLoop, calls=%fused_computation.3 | loop fusion | flops 18874368 | bytes 8388609 | tf_op jit(solution)/shard_map/jit(_where)/select_n | solution.py:491
  75.7 2.0 copy-done
  77.6 1.3 convolution_convert_fusion
  79.0 0.7 copy.13.down
  79.7 9.2 %collective-permute-done.6.two_a = bf16[1568,256]{1,0:T(8,128)(2,1)} collective-permute-done((bf16[1568,256]{1,0:T(8,128)(2,1)}, bf16[1568,256]{1,0:T(8,128)(2,1)}, u32[]{:S(2)}, u32[]{:S(2)}) %collective-permute-start.6) | collective-permute-done | bytes 802848 | tf_op jit(solution)/shard_map/ppermute | solution.py:464
  88.9 0.7 slice_bitcast_fusion.1
  89.6 0.6 pad_maximum_fusion.4.ups
  90.2 6.1 %project_line.1.so_far = f32[256,1024]{1,0:T(8,128)} custom-call(bf16[256,8192]{1,0:T(8,128)(2,1)} %copy-done, bf16[8192,128]{1,0:T(8,128)(2,1)} %own_key.5, bf16[8192,128]{1,0:T(8,128)(2,1)} %own_val.5, bf16[3104,256]{1,0:T(8,128)(2,1)} %copy-done.2, bf16[1568,256]{1,0:T(8,128)(2,1)} %collective-permute-done.6.two_a, ...), custom_call_target="tpu_custom_call" | custom-call | flops 1610612736 | bytes 8388608 | tf_op jit(solution)/shard_map/project_line/pallas_call | solution.py:137
  96.3 1.4 all-gather.3.cloned.1.call-done.far
  97.7 8.6 %project.1 = bf16[4,288,384]{2,1,0:T(8,128)(2,1)} custom-call(s32[2]{0:T(128)} %pad_add_fusion.place, bf16[256,8192]{1,0:T(8,128)(2,1)} %copy-done, bf16[8192,128]{1,0:T(8,128)(2,1)} %own_key.5, bf16[8192,128]{1,0:T(8,128)(2,1)} %own_val.5, bf16[5120,768]{1,0:T(8,128)(2,1)} %all-gather.3.cloned.1.call-done.far, f32[256,1024]{1,0:T(8,128)} %project_line.1.so_far, ...), custom_call_target="tpu_custom_call" | custom-call | flops 2684354560 | bytes 14680064 | tf_op jit(solution)/shard_map/project/pallas_call | solution.py:180
  106.3 4.7 %all-to-all-start = ((bf16[4,288,384]{2,1,0:T(8,128)(2,1)}), bf16[4,288,384]{2,1,0:T(8,128)(2,1)}, u32[]{:S(2)}, u32[]{:S(2)}) async-start(bf16[4,288,384]{2,1,0:T(8,128)(2,1)} %project.1), calls=%async_computation | async-start | bytes 1769472 | tf_op jit(solution)/shard_map/all_to_all | solution.py:504
  111.0 2.5 %pad_maximum_fusion = (f32[1024,128]{1,0:T(8,128)}, f32[1024,128]{1,0:T(8,128)}) fusion(f32[1024,64]{1,0:T(8,128)} %copy-done.9, f32[1024,64]{1,0:T(8,128)S(1)} %copy-done.6, f32[1024,64]{1,0:T(8,128)S(1)} %copy-done.8), kind=kLoop, calls=%fused_computation.14 | loop fusion | flops 262144 | bytes 1835008 | tf_op jit(solution)/shard_map/concatenate | solution.py:37
  113.5 2.3 %fusion.3 = f32[128]{0:T(128)S(1)} fusion(bf16[32,8192]{1,0:T(8,128)(2,1)} %factor.1, bf16[32,128]{1,0:T(8,128)(2,1)S(1)} %copy-done.14, bf16[8192,128]{1,0:T(8,128)(2,1)S(1)} %copy-done.1), kind=kOutput, calls=%fused_computation.6 | convolution fusion | flops 72351616 | bytes 2630144 | tf_op jit(solution)/shard_map/dot_general | solution.py:496
  115.9 0.5 fusion.14
  116.4 16.4 %all-to-all-done.rows = bf16[4,288,384]{2,1,0:T(8,128)(2,1)} async-done(((bf16[4,288,384]{2,1,0:T(8,128)(2,1)}), bf16[4,288,384]{2,1,0:T(8,128)(2,1)}, u32[]{:S(2)}, u32[]{:S(2)}) %all-to-all-start) | async-done | bytes 884768 | tf_op jit(solution)/shard_map/all_to_all | solution.py:504
  132.8 14.7 %attend.1 = (bf16[1024,256]{1,0:T(8,128)(2,1)}, f32[32,128]{1,0:T(8,128)}, f32[8,128]{1,0:T(8,128)}) custom-call(bf16[1024,512]{1,0:T(8,128)(2,1)} %query.1, bf16[1024,512]{1,0:T(8,128)(2,1)} %grad.1, bf16[4,288,384]{2,1,0:T(8,128)(2,1)} %all-to-all-done.rows, f32[1,128]{1,0:T(1,128)} %get-tuple-element.23.col_scale, f32[1024,128]{1,0:T(8,128)} %get-tuple-element.31.cos, ...), custom_call_target="tpu_custom_call" | custom-call | flops 5368709120 | bytes 6291456 | tf_op jit(solution)/shard_map/attend/pallas_call | solution.py:265
  147.5 3.5 %all-to-all-start.1 = ((bf16[4,256,256]{2,1,0:T(8,128)(2,1)}), bf16[4,256,256]{2,1,0:T(8,128)(2,1)S(1)}, u32[]{:S(2)}, u32[]{:S(2)}) async-start(bf16[4,256,256]{2,1,0:T(8,128)(2,1)} %bitcast.25), calls=%async_computation.1 | async-start | bytes 1048576 | tf_op jit(solution)/shard_map/all_to_all | solution.py:506
  151.0 0.0 all-gather.5.cloned.1.call-start
  151.1 0.7 broadcast_divide_fusion
  151.7 0.7 pad_maximum_fusion.5
  152.5 5.2 %collective-permute-start.10 = (f32[40,128]{1,0:T(8,128)S(1)}, f32[40,128]{1,0:T(8,128)S(1)}, u32[]{:S(2)}, u32[]{:S(2)}) collective-permute-start(f32[40,128]{1,0:T(8,128)S(1)} %pad_maximum_fusion.5), channel_id=1, source_target_pairs={{0,8},{8,0},{1,9},{9,1},{2,10},{10,2},{3,11},{11,3},{4,12},{12,4},... | collective-permute-start | bytes 61448 | tf_op jit(solution)/shard_map/ppermute | solution.py:508
  157.6 7.0 %collective-permute-done.10 = f32[40,128]{1,0:T(8,128)S(1)} collective-permute-done((f32[40,128]{1,0:T(8,128)S(1)}, f32[40,128]{1,0:T(8,128)S(1)}, u32[]{:S(2)}, u32[]{:S(2)}) %collective-permute-start.10) | collective-permute-done | bytes 20512 | tf_op jit(solution)/shard_map/ppermute | solution.py:508
  164.6 0.7 fusion.13
  165.3 0.6 pad.9._
  166.0 0.8 copy-done.4
  166.8 10.1 %back.1 = (bf16[128,8192]{1,0:T(8,128)(2,1)}, bf16[128,8192]{1,0:T(8,128)(2,1)}) custom-call(s32[2]{0:T(128)} %pad_add_fusion.place, bf16[4,256,256]{2,1,0:T(8,128)(2,1)} %copy-done.4, bf16[8192,128]{1,0:T(8,128)(2,1)} %own_key.5, bf16[8192,128]{1,0:T(8,128)(2,1)} %own_val.5, bf16[5120,768]{1,0:T(8,128)(2,1)} %all-gather.3.cloned.1.call-done.far, ...), custom_call_target="tpu_custom_call" | custom-call | flops 4294967296 | bytes 20971520 | tf_op jit(solution)/shard_map/back/pallas_call | solution.py:348
  176.9 2.8 %collective-permute-start.11 = (bf16[128,8192]{1,0:T(8,128)(2,1)}, bf16[128,8192]{1,0:T(8,128)(2,1)S(1)}, u32[]{:S(2)}, u32[]{:S(2)}) collective-permute-start(bf16[128,8192]{1,0:T(8,128)(2,1)} %get-tuple-element.16), channel_id=1, source_target_pairs={{0,1},{1,0},{2,3},{3,2},{4,5},{5,4},{6,7},{7,6},{8,9},{9,8},{10,11... | collective-permute-start | bytes 6291464 | tf_op jit(solution)/shard_map/ppermute | solution.py:514
  179.7 0.0 all-gather.5.cloned.1.call-update
  179.7 1.9 rank_part.1
  181.6 0.0 collective-permute-start.9
  181.6 2.2 collective-permute-done.9
  183.9 1.5 add_convert_fusion.rank
  185.4 4.6 %down_part.1 = bf16[1024,128]{1,0:T(8,128)(2,1)} custom-call(s32[2]{0:T(128)} %pad_add_fusion.place, bf16[256,32]{1,0:T(8,128)(2,1)} %add_convert_fusion.rank, bf16[256,8192]{1,0:T(8,128)(2,1)} %copy-done), custom_call_target="tpu_custom_call" | custom-call | flops 134217728 | bytes 5242880 | tf_op jit(solution)/shard_map/down_part/pallas_call | solution.py:425
  190.0 10.6 %all-to-all-start.2 = ((bf16[128,8,128]{2,1,0:T(8,128)(2,1)}), bf16[128,8,128]{2,1,0:T(8,128)(2,1)S(1)}, u32[]{:S(2)}, u32[]{:S(2)}) async-start(bf16[128,8,128]{2,1,0:T(8,128)(2,1)} %bitcast.22), calls=%async_computation.2 | async-start | bytes 524288 | tf_op jit(solution)/shard_map/all_to_all | solution.py:515
  200.6 1.3 copy-done.10
  202.0 5.2 %join.1._ = bf16[128,8192]{1,0:T(8,128)(2,1)} custom-call(s32[2]{0:T(128)} %pad_add_fusion.place, bf16[256,32]{1,0:T(8,128)(2,1)} %add_convert_fusion.rank, bf16[32,8192]{1,0:T(8,128)(2,1)} %factor.1, bf16[128,8192]{1,0:T(8,128)(2,1)} %get-tuple-element.15.mine, bf16[128,8192]{1,0:T(8,128)(2,1)} %copy-done.10), custom_call_target="tpu_custom_call" | custom-call | tf_op jit(solution)/shard_map/join/pallas_call | solution.py:393
  207.2 7.5 %all-to-all-done.2 = bf16[128,8,128]{2,1,0:T(8,128)(2,1)S(1)} async-done(((bf16[128,8,128]{2,1,0:T(8,128)(2,1)}), bf16[128,8,128]{2,1,0:T(8,128)(2,1)S(1)}, u32[]{:S(2)}, u32[]{:S(2)}) %all-to-all-start.2) | async-done | bytes 262176 | tf_op jit(solution)/shard_map/all_to_all | solution.py:515
  214.7 9.0 %all-gather.5.cloned.1.call-done = f32[2048,128]{1,0:T(8,128)} async-done(((f32[128,128]{1,0:T(8,128)}), f32[2048,128]{1,0:T(8,128)}) %all-gather.5.cloned.1.call-update) | async-done | bytes 1048592 | tf_op jit(solution)/shard_map/all_gather | solution.py:510
  223.7 1.9 finish.1
  225.6 1.2 slice_bitcast_fusion.3
  (44 shorter events, 0.1 us)
Async XLA Ops:
  7.2 20.5 %slice-start.1 = ((bf16[8192,128]{1,0:T(8,128)(2,1)}), bf16[3072,128]{1,0:T(8,128)(2,1)S(1)}, s32[]{:S(2)}) async-start(bf16[8192,128]{1,0:T(8,128)(2,1)} %own_val.5), calls=%async_computation.6 | async-start | bytes 1572864 | tf_op jit(solution)/shard_map/slice | solution.py:476
  7.2 20.5 %slice-start = ((bf16[8192,128]{1,0:T(8,128)(2,1)}), bf16[3072,128]{1,0:T(8,128)(2,1)S(1)}, s32[]{:S(2)}) async-start(bf16[8192,128]{1,0:T(8,128)(2,1)} %own_key.5), calls=%async_computation.5 | async-start | bytes 1572864 | tf_op jit(solution)/shard_map/slice | solution.py:476
  7.2 20.5 %copy-start.14 = (bf16[32,128]{1,0:T(8,128)(2,1)S(1)}, bf16[32,128]{1,0:T(8,128)(2,1)}, u32[]{:S(2)}) copy-start(bf16[32,128]{1,0:T(8,128)(2,1)} %param.12) | copy-start | bytes 24580
  7.2 90.5 %all-gather.3.cloned.1.call-start = ((), (), s32[]{:S(2)}) async-start(), calls=%async_computation.3 | async-start | bytes 8355840 | tf_op jit(solution)/shard_map/all_gather | solution.py:475
  8.3 14.3 %collective-permute-start.4 = (bf16[320,256]{1,0:T(8,128)(2,1)S(1)}, bf16[320,256]{1,0:T(8,128)(2,1)S(1)}, u32[]{:S(2)}, u32[]{:S(2)}) collective-permute-start(bf16[320,256]{1,0:T(8,128)(2,1)S(1)} %pad_maximum_fusion.3), channel_id=1, source_target_pairs={{0,2},{2,4},{4,6},{6,8},{8,10},{10,12},{12,14},{14,0},{1,3},{3,5},... | collective-permute-start | bytes 491528 | tf_op jit(solution)/shard_map/ppermute | solution.py:464
  10.9 11.8 %collective-permute-start.1 = (bf16[320,256]{1,0:T(8,128)(2,1)S(1)}, bf16[320,256]{1,0:T(8,128)(2,1)S(1)}, u32[]{:S(2)}, u32[]{:S(2)}) collective-permute-start(bf16[320,256]{1,0:T(8,128)(2,1)S(1)} %pad_maximum_fusion.3), channel_id=1, source_target_pairs={{0,14},{2,0},{4,2},{6,4},{8,6},{10,8},{12,10},{14,12},{1,15},{3,1}... | collective-permute-start | bytes 491528 | tf_op jit(solution)/shard_map/ppermute | solution.py:464
  14.9 5.7 %collective-permute-start.2 = (bf16[160,256]{1,0:T(8,128)(2,1)S(1)}, bf16[160,256]{1,0:T(8,128)(2,1)S(1)}, u32[]{:S(2)}, u32[]{:S(2)}) collective-permute-start(bf16[160,256]{1,0:T(8,128)(2,1)S(1)} %get-tuple-element.20), channel_id=1, source_target_pairs={{0,12},{2,14},{4,0},{6,2},{8,4},{10,6},{12,8},{14,10},{1,13},{3,15... | collective-permute-start | bytes 245768 | tf_op jit(solution)/shard_map/ppermute | solution.py:464
  16.8 5.8 %collective-permute-start.3 = (bf16[160,256]{1,0:T(8,128)(2,1)S(1)}, bf16[160,256]{1,0:T(8,128)(2,1)S(1)}, u32[]{:S(2)}, u32[]{:S(2)}) collective-permute-start(bf16[160,256]{1,0:T(8,128)(2,1)S(1)} %get-tuple-element.21), channel_id=1, source_target_pairs={{0,4},{2,6},{4,8},{6,10},{8,12},{10,14},{12,0},{14,2},{1,5},{3,7},... | collective-permute-start | bytes 245768 | tf_op jit(solution)/shard_map/ppermute | solution.py:464
  23.5 48.9 %collective-permute-start = (bf16[128,8192]{1,0:T(8,128)(2,1)}, bf16[128,8192]{1,0:T(8,128)(2,1)}, u32[]{:S(2)}, u32[]{:S(2)}) collective-permute-start(bf16[128,8192]{1,0:T(8,128)(2,1)} %param.8), channel_id=1, source_target_pairs={{0,1},{1,0},{2,3},{3,2},{4,5},{5,4},{6,7},{7,6},{8,9},{9,8},{10,11... | collective-permute-start | bytes 6291464 | tf_op jit(solution)/shard_map/ppermute | solution.py:490
  29.8 37.9 %collective-permute-start.7 = (bf16[3104,256]{1,0:T(8,128)(2,1)}, bf16[3104,256]{1,0:T(8,128)(2,1)S(1)}, u32[]{:S(2)}, u32[]{:S(2)}) collective-permute-start(bf16[3104,256]{1,0:T(8,128)(2,1)} %fusion.5), channel_id=1, source_target_pairs={{0,2},{2,4},{4,6},{6,8},{8,10},{10,12},{12,14},{14,0},{1,3},{3,5},... | collective-permute-start | bytes 4767752 | tf_op jit(solution)/shard_map/ppermute | solution.py:464
  29.9 38.8 %collective-permute-start.5 = (bf16[3104,256]{1,0:T(8,128)(2,1)}, bf16[3104,256]{1,0:T(8,128)(2,1)S(1)}, u32[]{:S(2)}, u32[]{:S(2)}) collective-permute-start(bf16[3104,256]{1,0:T(8,128)(2,1)} %fusion.5), channel_id=1, source_target_pairs={{0,14},{2,0},{4,2},{6,4},{8,6},{10,8},{12,10},{14,12},{1,15},{3,1}... | collective-permute-start | bytes 4767752 | tf_op jit(solution)/shard_map/ppermute | solution.py:464
  33.1 39.3 %copy-start.11 = (bf16[128,8192]{1,0:T(8,128)(2,1)S(1)}, bf16[128,8192]{1,0:T(8,128)(2,1)}, u32[]{:S(2)}) copy-start(bf16[128,8192]{1,0:T(8,128)(2,1)} %param.8) | copy-start | bytes 6291460
  35.1 0.8 copy-start.5
  35.1 1.6 copy-start.7
  35.1 1.6 copy-start.9
  67.6 8.0 %copy-start.3 = (bf16[3104,256]{1,0:T(8,128)(2,1)}, bf16[3104,256]{1,0:T(8,128)(2,1)S(1)}, u32[]{:S(2)}) copy-start(bf16[3104,256]{1,0:T(8,128)(2,1)S(1)} %collective-permute-done.7.three) | copy-start | bytes 4767748
  68.7 21.5 %collective-permute-start.8 = (bf16[1536,256]{1,0:T(8,128)(2,1)}, bf16[1536,256]{1,0:T(8,128)(2,1)}, u32[]{:S(2)}, u32[]{:S(2)}) collective-permute-start(bf16[1536,256]{1,0:T(8,128)(2,1)} %slice.49), channel_id=1, source_target_pairs={{0,2},{2,4},{4,6},{6,8},{8,10},{10,12},{12,14},{14,0},{1,3},{3,5},... | collective-permute-start | bytes 2359304 | tf_op jit(solution)/shard_map/ppermute | solution.py:464
  68.7 7.0 %copy-start.2 = (bf16[3104,256]{1,0:T(8,128)(2,1)}, bf16[3104,256]{1,0:T(8,128)(2,1)S(1)}, u32[]{:S(2)}) copy-start(bf16[3104,256]{1,0:T(8,128)(2,1)S(1)} %collective-permute-done.5.one) | copy-start | bytes 4767748
  69.7 19.2 %collective-permute-start.6 = (bf16[1568,256]{1,0:T(8,128)(2,1)}, bf16[1568,256]{1,0:T(8,128)(2,1)}, u32[]{:S(2)}, u32[]{:S(2)}) collective-permute-start(bf16[1568,256]{1,0:T(8,128)(2,1)} %slice.48), channel_id=1, source_target_pairs={{0,14},{2,0},{4,2},{6,4},{8,6},{10,8},{12,10},{14,12},{1,15},{3,1}... | collective-permute-start | bytes 2408456 | tf_op jit(solution)/shard_map/ppermute | solution.py:464
  72.4 5.3 %copy-start.12 = (bf16[32,8192]{1,0:T(8,128)(2,1)S(1)}, bf16[32,8192]{1,0:T(8,128)(2,1)}, u32[]{:S(2)}) copy-start(bf16[32,8192]{1,0:T(8,128)(2,1)} %factor.1) | copy-start | bytes 1572868
  75.7 2.0 copy-start
  97.7 13.3 %copy-start.6 = (f32[1024,64]{1,0:T(8,128)S(1)}, f32[1024,64]{1,0:T(8,128)}, u32[]{:S(2)}) copy-start(f32[1024,64]{1,0:T(8,128)} %copy-done.5) | copy-start | bytes 786436
  97.7 13.3 %copy-start.8 = (f32[1024,64]{1,0:T(8,128)S(1)}, f32[1024,64]{1,0:T(8,128)}, u32[]{:S(2)}) copy-start(f32[1024,64]{1,0:T(8,128)} %copy-done.7) | copy-start | bytes 786436
  106.3 7.2 %copy-start.1 = (bf16[8192,128]{1,0:T(8,128)(2,1)S(1)}, bf16[8192,128]{1,0:T(8,128)(2,1)}, u32[]{:S(2)}) copy-start(bf16[8192,128]{1,0:T(8,128)(2,1)} %own_val.5) | copy-start | bytes 6291460
  106.3 26.5 %all-to-all-start = ((bf16[4,288,384]{2,1,0:T(8,128)(2,1)}), bf16[4,288,384]{2,1,0:T(8,128)(2,1)}, u32[]{:S(2)}, u32[]{:S(2)}) async-start(bf16[4,288,384]{2,1,0:T(8,128)(2,1)} %project.1), calls=%async_computation | async-start | bytes 1769472 | tf_op jit(solution)/shard_map/all_to_all | solution.py:504
  113.5 2.3 %copy-start.15 = (f32[128]{0:T(128)S(1)}, f32[128]{0:T(128)}, u32[]{:S(2)}) copy-start(f32[128]{0:T(128)} %param.13) | copy-start | bytes 1540
  147.5 18.4 %all-to-all-start.1 = ((bf16[4,256,256]{2,1,0:T(8,128)(2,1)}), bf16[4,256,256]{2,1,0:T(8,128)(2,1)S(1)}, u32[]{:S(2)}, u32[]{:S(2)}) async-start(bf16[4,256,256]{2,1,0:T(8,128)(2,1)} %bitcast.25), calls=%async_computation.1 | async-start | bytes 1048576 | tf_op jit(solution)/shard_map/all_to_all | solution.py:506
  151.0 72.7 %all-gather.5.cloned.1.call-start = ((), (), s32[]{:S(2)}) async-start(), calls=%async_computation.4 | async-start | bytes 1114112 | tf_op jit(solution)/shard_map/all_gather | solution.py:510
  152.5 12.1 %collective-permute-start.10 = (f32[40,128]{1,0:T(8,128)S(1)}, f32[40,128]{1,0:T(8,128)S(1)}, u32[]{:S(2)}, u32[]{:S(2)}) collective-permute-start(f32[40,128]{1,0:T(8,128)S(1)} %pad_maximum_fusion.5), channel_id=1, source_target_pairs={{0,8},{8,0},{1,9},{9,1},{2,10},{10,2},{3,11},{11,3},{4,12},{12,4},... | collective-permute-start | bytes 61448 | tf_op jit(solution)/shard_map/ppermute | solution.py:508
  166.0 0.8 copy-start.4
  176.9 23.7 %collective-permute-start.11 = (bf16[128,8192]{1,0:T(8,128)(2,1)}, bf16[128,8192]{1,0:T(8,128)(2,1)S(1)}, u32[]{:S(2)}, u32[]{:S(2)}) collective-permute-start(bf16[128,8192]{1,0:T(8,128)(2,1)} %get-tuple-element.16), channel_id=1, source_target_pairs={{0,1},{1,0},{2,3},{3,2},{4,5},{5,4},{6,7},{7,6},{8,9},{9,8},{10,11... | collective-permute-start | bytes 6291464 | tf_op jit(solution)/shard_map/ppermute | solution.py:514
  181.6 2.3 collective-permute-start.9
  190.0 24.7 %all-to-all-start.2 = ((bf16[128,8,128]{2,1,0:T(8,128)(2,1)}), bf16[128,8,128]{2,1,0:T(8,128)(2,1)S(1)}, u32[]{:S(2)}, u32[]{:S(2)}) async-start(bf16[128,8,128]{2,1,0:T(8,128)(2,1)} %bitcast.22), calls=%async_computation.2 | async-start | bytes 524288 | tf_op jit(solution)/shard_map/all_to_all | solution.py:515
  200.6 1.3 copy-start.10
  214.7 9.0 %copy-start.13 = (bf16[128,8,128]{2,1,0:T(8,128)(2,1)}, bf16[128,8,128]{2,1,0:T(8,128)(2,1)S(1)}, u32[]{:S(2)}) copy-start(bf16[128,8,128]{2,1,0:T(8,128)(2,1)S(1)} %all-to-all-done.2) | copy-start | bytes 786436
Sparse Core Ops, SparseCore 0:
  23.6 74.0 all-gather.2
  179.8 43.8 all-gather.4
where the time goes:
time: 235 us; the launch traced here: 234 us
  waiting for transfers between devices  89 us (38%)
  Pallas kernels  53.1 us (23%)
  starting transfers between devices  44.1 us (19%)
  other arithmetic  18.1 us (8%)
  between operations  14.3 us (6%)
  local copies, waits for them, and re-layouts  11.3 us (5%)
  matrix products  3.69 us (2%)
    ppermute x8, waiting for transfers between devices, along_z(): lax.ppermute(value, ('zh', 'zl'), [(i, (i + shift) % 8) for i in range(8)])  45.4 us
    all_to_all x1, waiting for transfers between devices, shards(): rows = lax.all_to_all(rows, 'zl', 0, 0, tiled=True)  16.4 us
    pallas_call x1, Pallas kernels, attend(): pl.pallas_call(attend_kernel, grid=(GROUP,), in_specs=[pl.BlockSpec((SEQ,...  14.7 us
    ppermute x8, starting transfers between devices, along_z(): lax.ppermute(value, ('zh', 'zl'), [(i, (i + shift) % 8) for i in range(8)])  14.4 us
    all_to_all x1, starting transfers between devices, shards(): lax.all_to_all(down_part(place, rank, pair), DP + ('zl',), 0, 0, tiled=True)  10.6 us
    pallas_call x1, Pallas kernels, back(): pl.pallas_call(back_kernel, in_specs=[smem(), whole((4, PAIR, 2 * HD))] +...  10.1 us
    all_gather x1, waiting for transfers between devices, shards(): small = lax.all_gather(padded, ('x', 'y'), axis=0, tiled=True)  9.03 us
    pallas_call x1, Pallas kernels, project(): pl.pallas_call(project_kernel, in_specs=[smem(), any_ref(), any_ref(), an...  8.62 us
  transfers between devices with their start and end apart: 17, of which 10 were waited for; matrix products, arithmetic and copies ran while one was open for 11% of the time, Pallas kernels for 8%

commit v1 on v0

--- a/solution.py
+++ b/solution.py
@@ -16,6 +16,8 @@
 CHUNK = 1280
 QB = 256
 GROUP = 4
+HEADS = 2
+SMALL = 256
 SCALE = 2.0
 ROPE_BASE = 500000.0
 LOG2E = 1.4426950408889634
@@ -205,10 +207,10 @@
     )(place, pair, w_key, w_val, far, so_far, down, ups, cos, sin)
 
 
-def attend_kernel(query, grad, rows, col_scale, cos, sin, grads, up_grad, mag_grad, keys, vals, dkey, dval):
-    head = pl.program_id(0)
-
-    @pl.when(head == 0)
+def attend_kernel(query, grad, rows, col_scale, norms, cos, sin, grads, small, keys, vals, dkey, dval):
+    step = pl.program_id(0)
+
+    @pl.when(step == 0)
     def _():
         for i in range(4):
             here = slice(i * PAIR, (i + 1) * PAIR)
@@ -220,27 +222,36 @@
     for block in range(SEQ // QB):
         stop = (block + 1) * QB
         here = slice(block * QB, stop)
-        q = query[here, :]
-        g = grad[here, :]
-        qq = jnp.concatenate([q, q], axis=1)
-        scores = lax.dot_general(keys[:stop], qq, NT, preferred_element_type=F32)
-        key_at = lax.broadcasted_iota(jnp.int32, (QB, QB), 0)
-        query_at = lax.broadcasted_iota(jnp.int32, (QB, QB), 1)
-        edge = jnp.where(key_at <= query_at, scores[block * QB :], -1e30)
-        if block:
-            scores = jnp.concatenate([scores[: block * QB], edge], axis=0)
-        else:
-            scores = edge
-        powers = jnp.exp2(scores - jnp.max(scores, axis=0, keepdims=True))
-        attn = powers * (1.0 / jnp.sum(powers, axis=0, keepdims=True))
-        half = attn.astype(BF)
-        pgrad = lax.dot_general(vals[:stop], g, NT, preferred_element_type=F32)
-        delta = jnp.sum(half.astype(F32) * pgrad, axis=0, keepdims=True)
-        sgrad = (attn * (pgrad - delta)).astype(BF)
-        dval[:stop] += jnp.dot(half, g, preferred_element_type=F32)
-        dkey[:stop] += jnp.dot(sgrad, q, preferred_element_type=F32)
-
-    @pl.when(head == pl.num_programs(0) - 1)
+        queries, outs, halves, sgrads = [], [], [], []
+        for head in range(HEADS):
+            q = query[here, head * HD : (head + 1) * HD]
+            g = grad[here, head * HD : (head + 1) * HD]
+            qq = jnp.concatenate([q, q], axis=1)
+            scores = lax.dot_general(keys[:stop], qq, NT, preferred_element_type=F32)
+            key_at = lax.broadcasted_iota(jnp.int32, (QB, QB), 0)
+            query_at = lax.broadcasted_iota(jnp.int32, (QB, QB), 1)
+            edge = jnp.where(key_at <= query_at, scores[block * QB :], -1e30)
+            if block:
+                scores = jnp.concatenate([scores[: block * QB], edge], axis=0)
+            else:
+                scores = edge
+            powers = jnp.exp2(scores - jnp.max(scores, axis=0, keepdims=True))
+            attn = powers * (1.0 / jnp.sum(powers, axis=0, keepdims=True))
+            half = attn.astype(BF)
+            pgrad = lax.dot_general(vals[:stop], g, NT, preferred_element_type=F32)
+            delta = jnp.sum(half.astype(F32) * pgrad, axis=0, keepdims=True)
+            sgrads.append((attn * (pgrad - delta)).astype(BF))
+            halves.append(half)
+            queries.append(q)
+            outs.append(g)
+        dval[:stop] += jnp.dot(
+            jnp.concatenate(halves, 1), jnp.concatenate(outs, 0), preferred_element_type=F32
+        )
+        dkey[:stop] += jnp.dot(
+            jnp.concatenate(sgrads, 1), jnp.concatenate(queries, 0), preferred_element_type=F32
+        )
+
+    @pl.when(step == pl.num_programs(0) - 1)
     def _():
         dk = dkey[...] * INV_SQRT
         dk = dk * cos[...] - pltpu.roll(dk, HD // 2, 1) * sin[...]
@@ -257,28 +268,25 @@
             down = jnp.concatenate([packed[:, 32 * j : 32 * j + 32] for j in range(4)], axis=0)
             total += lax.dot_general(down, gv[here], TN, preferred_element_type=F32)
             mags += jnp.sum(dv[here] * rows[i, :PAIR, 2 * HD :].astype(F32), axis=0, keepdims=True)
-        up_grad[...] = SCALE * total
-        mag_grad[...] = jnp.broadcast_to(mags, mag_grad.shape)
-
-
-def attend(queries, grad_attn, rows, col_scale, cos, sin):
+        small[:RANK, :] = SCALE * total
+        small[RANK:, :] = jnp.broadcast_to(mags / norms[...], (SMALL - RANK, HD))
+
+
+def attend(queries, grad_attn, rows, col_scale, norms, cos, sin):
     return pl.pallas_call(
         attend_kernel,
-        grid=(GROUP,),
+        grid=(GROUP // HEADS,),
         in_specs=[
-            pl.BlockSpec((SEQ, HD), lambda h: (0, h)),
-            pl.BlockSpec((SEQ, HD), lambda h: (0, h)),
+            pl.BlockSpec((SEQ, HEADS * HD), lambda h: (0, h)),
+            pl.BlockSpec((SEQ, HEADS * HD), lambda h: (0, h)),
             whole((4, PAIR + 32, 3 * HD)),
+            whole((1, HD)),
             whole((1, HD)),
             whole((SEQ, HD)),
             whole((SEQ, HD)),
         ],
-        out_specs=[whole((SEQ, 2 * HD)), whole((RANK, HD)), whole((8, HD))],
-        out_shape=[
-            jax.ShapeDtypeStruct((SEQ, 2 * HD), BF),
-            jax.ShapeDtypeStruct((RANK, HD), F32),
-            jax.ShapeDtypeStruct((8, HD), F32),
-        ],
+        out_specs=[whole((SEQ, 2 * HD)), whole((SMALL, HD))],
+        out_shape=[jax.ShapeDtypeStruct((SEQ, 2 * HD), BF), jax.ShapeDtypeStruct((SMALL, HD), F32)],
         scratch_shapes=[
             pltpu.VMEM((SEQ, 2 * HD), BF),
             pltpu.VMEM((SEQ, HD), BF),
@@ -288,7 +296,7 @@
         compiler_params=params(60),
         cost_estimate=cost(5 * 2 * GROUP * SEQ * SEQ * HD, 6 * MIB, GROUP * SEQ * SEQ),
         name="attend",
-    )(queries, grad_attn, rows, col_scale, cos, sin)
+    )(queries, grad_attn, rows, col_scale, norms, cos, sin)
 
 
 def rank_kernel(place, grads, ups, out):
@@ -359,12 +367,12 @@
             pltpu.SemaphoreType.DMA((2, count + 2)),
         ],
         compiler_params=params(60),
-        cost_estimate=cost(2 * PAIR * D * 1024, 20 * MIB),
+        cost_estimate=cost(0, 0),
         name="back",
     )(place, grads, w_key, w_val, far, *line, after)
 
 
-def join_kernel(place, rank, factor, mine, theirs, out, one, two, result, sems, out_sem):
+def join_kernel(place, rank, factor, mine, theirs, _, out, one, two, result, sems, out_sem):
     size = D // 8
     chunks = []
     for i in range(8):
@@ -389,10 +397,10 @@
     wait_all(leaving)
 
 
-def join(place, rank, factor, mine, theirs):
+def join(place, rank, factor, mine, theirs, after):
     return pl.pallas_call(
         join_kernel,
-        in_specs=[smem(), whole((PAIR, RANK)), whole((RANK, D)), any_ref(), any_ref()],
+        in_specs=[smem(), whole((PAIR, RANK)), whole((RANK, D))] + [any_ref()] * 3,
         out_specs=any_ref(),
         out_shape=jax.ShapeDtypeStruct((128, D), BF),
         scratch_shapes=[pltpu.VMEM((128, D), BF)] * 3
@@ -400,15 +408,16 @@
         compiler_params=params(60),
         cost_estimate=cost(0, 0),
         name="join",
-    )(place, rank, factor, mine, theirs)
-
-
-def down_kernel(place, rank, hid, out):
-    part = SCALE * lax.dot_general(rank[...], hid[...], TN, preferred_element_type=F32)
+    )(place, rank, factor, mine, theirs, after)
+
+
+def down_kernel(place, part, got, hid, out, rank):
+    rank[...] = (part[...] + got[...]).astype(BF)
+    product = SCALE * lax.dot_general(rank[...], hid[...], TN, preferred_element_type=F32)
     lane = lax.broadcasted_iota(jnp.int32, (8, HD), 1) // 32
     core = place[1]
-    for tile in range(part.shape[1] // HD):
-        regs = [part[8 * i : 8 * i + 8, tile * HD : (tile + 1) * HD] for i in range(4)]
+    for tile in range(product.shape[1] // HD):
+        regs = [product[8 * i : 8 * i + 8, tile * HD : (tile + 1) * HD] for i in range(4)]
         blocks = []
         for pick in range(2):
             column = 2 * pick + core
@@ -420,34 +429,55 @@
         out[16 * tile : 16 * tile + 16, :] = jnp.concatenate(blocks, axis=0).astype(BF)
 
 
-def down_part(place, rank, pair):
+def down_part(place, part, got, pair):
     wide = 2048
     return pl.pallas_call(
         down_kernel,
         grid=(D // wide,),
-        in_specs=[smem(), whole((PAIR, RANK)), pl.BlockSpec((PAIR, wide), lambda k: (0, k))],
-        out_specs=pl.BlockSpec((wide // 8, HD), lambda k: (k, 0)),
-        out_shape=jax.ShapeDtypeStruct((1024, HD), BF),
+        in_specs=[
+            smem(),
+            whole((PAIR, RANK)),
+            whole((PAIR, RANK)),
+            pl.BlockSpec((PAIR, wide), lambda k: (0, k)),
+        ],
+        out_specs=[pl.BlockSpec((wide // 8, HD), lambda k: (k, 0)), whole((PAIR, RANK))],
+        out_shape=[jax.ShapeDtypeStruct((1024, HD), BF), jax.ShapeDtypeStruct((PAIR, RANK), BF)],
         compiler_params=params(60),
         cost_estimate=cost(2 * PAIR * D * RANK, 5 * MIB),
         name="down_part",
-    )(place, rank, pair)
-
-
-def finish_kernel(pieces, small, _, out, up_grad, mag_grad):
+    )(place, part, got, pair)
+
+
+def fold_kernel(small, out):
+    out[...] = jnp.sum(small[...], axis=0)
+
+
+def fold(small):
+    return pl.pallas_call(
+        fold_kernel,
+        grid=(1,),
+        in_specs=[whole((16, 40, HD))],
+        out_specs=whole((40, HD)),
+        out_shape=jax.ShapeDtypeStruct((40, HD), F32),
+        compiler_params=params(60),
+        cost_estimate=cost(0, 0),
+        name="fold",
+    )(small)
+
+
+def finish_kernel(pieces, small, other, _, out, up_grad, mag_grad):
     total = jnp.sum(pieces[...].astype(F32).reshape(128, 8, HD), axis=0)
     for i in range(4):
         out[8 * i : 8 * i + 8, :] = total[:, 32 * i : 32 * i + 32]
-    sums = jnp.sum(small[...], axis=0)
+    sums = small[...] + other[...]
     up_grad[...] = sums[:RANK]
     mag_grad[...] = sums[RANK:]
 
 
-def finish(pieces, small, after):
+def finish(pieces, small, other, after):
     return pl.pallas_call(
         finish_kernel,
-        grid=(1,),
-        in_specs=[whole((1024, HD)), whole((16, 40, HD)), any_ref()],
+        in_specs=[whole((1024, HD)), whole((40, HD)), whole((40, HD)), any_ref()],
         out_specs=[whole((RANK, 32)), whole((RANK, HD)), whole((8, HD))],
         out_shape=[
             jax.ShapeDtypeStruct((RANK, 32), F32),
@@ -457,7 +487,7 @@
         compiler_params=params(60),
         cost_estimate=cost(0, 0),
         name="finish",
-    )(pieces, small, after)
+    )(pieces, small, other, after)
 
 
 def along_z(value, shift):
@@ -502,19 +532,19 @@
     so_far = project_line(pair, w_key, w_val, line)
     rows = project(place, pair, w_key, w_val, far, so_far, down, ups, cos_here, sin_here)
     rows = lax.all_to_all(rows, "zl", 0, 0, tiled=True)
-    grads, up_grad, mag_grad = attend(queries, grad_attn, rows, col_scale, cos, sin)
+    grads, small = attend(queries, grad_attn, rows, col_scale, norms.reshape(1, HD), cos, sin)
     grads = lax.all_to_all(grads.reshape(4, PAIR, 2 * HD), "zl", 0, 0, tiled=True)
-    small = jnp.concatenate([up_grad, mag_grad / norms], axis=0)
-    small = small + lax.ppermute(small, "zh", swap)
-    padded = jnp.pad(small, ((0, 88), (0, 0)))
-    small = lax.all_gather(padded, ("x", "y"), axis=0, tiled=True)
+    gathered = lax.all_gather(small, ("x", "y"), axis=0, tiled=True)
     part = rank_part(place, grads, ups)
-    rank = (part + lax.ppermute(part, "core", swap)).astype(BF)
-    mine, theirs = back(place, grads, w_key, w_val, far, line, padded)
+    got = lax.ppermute(part, "core", swap)
+    mine, theirs = back(place, grads, w_key, w_val, far, line, small)
     theirs = lax.ppermute(theirs, "core", swap)
-    pieces = lax.all_to_all(down_part(place, rank, pair), DP + ("zl",), 0, 0, tiled=True)
-    grad_hidden = join(place, rank, factor, mine, theirs)
-    grad_down, up_sum, mag_sum = finish(pieces, small.reshape(16, HD, HD), grad_hidden)
+    pieces, rank = down_part(place, part, got, pair)
+    pieces = lax.all_to_all(pieces, DP + ("zl",), 0, 0, tiled=True)
+    small = fold(gathered.reshape(16, SMALL, HD))
+    other = lax.ppermute(small, "zh", swap)
+    grad_hidden = join(place, rank, factor, mine, theirs, small)
+    grad_down, up_sum, mag_sum = finish(pieces, small, other, grad_hidden)
     return grad_hidden, grad_down, up_sum, mag_sum[0]
 
 

time: 235 us -> 222 us (0.945)
  waiting for transfers between devices: 89 us -> 68.2 us
  blocking collectives: 0 us -> 17.9 us
  starting transfers between devices: 44.1 us -> 39.5 us
  other arithmetic: 18.1 us -> 13.8 us
    all_to_all x0 -> x1, blocking collectives: none -> 17.9 us  [shards(): lax.all_to_all(grads.reshape(4, PAIR, 2 * HD), 'zl', 0, 0, tiled=True)]
    all_gather x1, waiting for transfers between devices: 9.03 us -> 0.02 us  [shards(): gathered = lax.all_gather(small, ('x', 'y'), axis=0, tiled=True)]
    ppermute x2, waiting for transfers between devices: 9.22 us -> 2.26 us  [the longest x1 2.26 us: shards(): got = lax.ppermute(part, 'core', swap)]
    all_to_all x2 -> x1, waiting for transfers between devices: 7.46 us -> 1.4 us  [shards(): pieces = lax.all_to_all(pieces, DP + ('zl',), 0, 0, tiled=True)]
    all_gather x1, waiting for transfers between devices: 1.37 us -> 4.26 us  [gather_weights(): lax.all_gather(jnp.concatenate([first, second, third], axis=1), ('x', 'y'...]
    all_to_all x2 -> x1, starting transfers between devices: 14.1 us -> 12 us  [shards(): pieces = lax.all_to_all(pieces, DP + ('zl',), 0, 0, tiled=True)]
    pallas_call x2 -> x3, Pallas kernels: 16.6 us -> 15.4 us  [the longest x1 12 us: attend(): pl.pallas_call(attend_kernel, grid=(GROUP // HEADS,), in_specs=[pl.BlockS...]
    unnamed x32 -> x36, local copies, waits for them, and re-layouts: 4.9 us -> 5.51 us
  transfers between devices with their start and end apart: 17 -> 16, of which waited for: 10 -> 8; matrix products, arithmetic and copies ran while one was open for 11% -> 9% of each run, Pallas kernels for 8% -> 13%
where the time goes in v1:
time: 222 us; the launch traced here: 221 us
  waiting for transfers between devices  68.2 us (31%)
  Pallas kernels  52.3 us (24%)
  starting transfers between devices  39.5 us (18%)
  blocking collectives  17.9 us (8%)
  between operations  14.3 us (6%)
  other arithmetic  13.8 us (6%)
  local copies, waits for them, and re-layouts  11.3 us (5%)
  matrix products  3.69 us (2%)
    ppermute x8, waiting for transfers between devices, along_z(): lax.ppermute(value, ('zh', 'zl'), [(i, (i + shift) % 8) for i in range(8)])  43.9 us
    all_to_all x1, blocking collectives, shards(): lax.all_to_all(grads.reshape(4, PAIR, 2 * HD), 'zl', 0, 0, tiled=True)  17.9 us
    all_to_all x1, waiting for transfers between devices, shards(): rows = lax.all_to_all(rows, 'zl', 0, 0, tiled=True)  16.4 us
    ppermute x8, starting transfers between devices, along_z(): lax.ppermute(value, ('zh', 'zl'), [(i, (i + shift) % 8) for i in range(8)])  14.5 us
    all_to_all x1, starting transfers between devices, shards(): pieces = lax.all_to_all(pieces, DP + ('zl',), 0, 0, tiled=True)  12 us
    pallas_call x1, Pallas kernels, attend(): pl.pallas_call(attend_kernel, grid=(GROUP // HEADS,), in_specs=[pl.BlockS...  12 us
    pallas_call x1, Pallas kernels, back(): pl.pallas_call(back_kernel, in_specs=[smem(), whole((4, PAIR, 2 * HD))] +...  10.1 us
    pallas_call x1, Pallas kernels, project(): pl.pallas_call(project_kernel, in_specs=[smem(), any_ref(), any_ref(), an...  8.63 us
  transfers between devices with their start and end apart: 16, of which 8 were waited for; matrix products, arithmetic and copies ran while one was open for 9% of the time, Pallas kernels for 13%

profile of v1, /device:TPU:1, one launch (start us, length us, event | category | flops | bytes accessed | tf_op | source)
XLA Modules:
  0.0 221.1 jit_solution(4734305588558846878)
XLA Ops:
  7.2 0.0 copy-start.1
  7.2 0.0 slice-start
  7.2 0.0 all-gather.3.cloned.1.call-start
  7.2 1.1 constant_dynamic-slice_fusion.1
  8.4 2.5 %collective-permute-start.4 = (bf16[320,256]{1,0:T(8,128)(2,1)S(1)}, bf16[320,256]{1,0:T(8,128)(2,1)S(1)}, u32[]{:S(2)}, u32[]{:S(2)}) collective-permute-start(bf16[320,256]{1,0:T(8,128)(2,1)S(1)} %pad_maximum_fusion.3), channel_id=1, source_target_pairs={{0,2},{2,4},{4,6},{6,8},{8,10},{10,12},{12,14},{14,0},{1,3},{3,5},... | collective-permute-start | bytes 491528 | tf_op jit(solution)/shard_map/ppermute | solution.py:494
  10.9 4.0 %collective-permute-start.1 = (bf16[320,256]{1,0:T(8,128)(2,1)S(1)}, bf16[320,256]{1,0:T(8,128)(2,1)S(1)}, u32[]{:S(2)}, u32[]{:S(2)}) collective-permute-start(bf16[320,256]{1,0:T(8,128)(2,1)S(1)} %pad_maximum_fusion.3), channel_id=1, source_target_pairs={{0,14},{2,0},{4,2},{6,4},{8,6},{10,8},{12,10},{14,12},{1,15},{3,1}... | collective-permute-start | bytes 491528 | tf_op jit(solution)/shard_map/ppermute | solution.py:494
  15.0 0.1 collective-permute-start.3
  15.1 3.6 %collective-permute-start.2 = (bf16[160,256]{1,0:T(8,128)(2,1)S(1)}, bf16[160,256]{1,0:T(8,128)(2,1)S(1)}, u32[]{:S(2)}, u32[]{:S(2)}) collective-permute-start(bf16[160,256]{1,0:T(8,128)(2,1)S(1)} %get-tuple-element.22), channel_id=1, source_target_pairs={{0,12},{2,14},{4,0},{6,2},{8,4},{10,6},{12,8},{14,10},{1,13},{3,15... | collective-permute-start | bytes 245768 | tf_op jit(solution)/shard_map/ppermute | solution.py:494
  18.6 3.8 %collective-permute-done.3 = bf16[160,256]{1,0:T(8,128)(2,1)S(1)} collective-permute-done((bf16[160,256]{1,0:T(8,128)(2,1)S(1)}, bf16[160,256]{1,0:T(8,128)(2,1)S(1)}, u32[]{:S(2)}, u32[]{:S(2)}) %collective-permute-start.3) | collective-permute-done | bytes 81952 | tf_op jit(solution)/shard_map/ppermute | solution.py:494
  22.4 0.8 pad_maximum_fusion.2
  23.2 0.0 all-gather.3.cloned.1.call-update
  23.3 0.0 slice-start.1
  23.3 2.0 collective-permute-start
  25.2 0.5 fusion.13
  25.8 2.1 fusion.5
  27.9 1.2 collective-permute-start.5
  29.0 0.3 collective-permute-start.7
  29.3 0.6 pad_add_fusion.place
  29.9 2.0 fusion.6
  31.9 0.8 copy-done.5
  32.7 0.8 fusion.9
  33.5 30.3 %collective-permute-done.5.one = bf16[3104,256]{1,0:T(8,128)(2,1)S(1)} collective-permute-done((bf16[3104,256]{1,0:T(8,128)(2,1)}, bf16[3104,256]{1,0:T(8,128)(2,1)S(1)}, u32[]{:S(2)}, u32[]{:S(2)}) %collective-permute-start.5) | collective-permute-done | bytes 1589280 | tf_op jit(solution)/shard_map/ppermute | solution.py:494
  63.9 1.1 slice.48
  64.9 2.4 %collective-permute-start.6 = (bf16[1568,256]{1,0:T(8,128)(2,1)}, bf16[1568,256]{1,0:T(8,128)(2,1)}, u32[]{:S(2)}, u32[]{:S(2)}) collective-permute-start(bf16[1568,256]{1,0:T(8,128)(2,1)} %slice.48), channel_id=1, source_target_pairs={{0,14},{2,0},{4,2},{6,4},{8,6},{10,8},{12,10},{14,12},{1,15},{3,1}... | collective-permute-start | bytes 2408456 | tf_op jit(solution)/shard_map/ppermute | solution.py:494
  67.3 1.0 slice.49
  68.3 0.4 collective-permute-start.8
  68.8 3.3 %maximum_select_fusion.pair.hid = bf16[256,8192]{1,0:T(8,128)(2,1)S(1)} fusion(bf16[128,8192]{1,0:T(8,128)(2,1)} %collective-permute-done, bf16[128,8192]{1,0:T(8,128)(2,1)S(1)} %copy-done.12, pred[]{:T(512)S(6)} %eq.3), kind=kLoop, calls=%fused_computation.3 | loop fusion | flops 18874368 | bytes 8388609 | tf_op jit(solution)/shard_map/jit(_where)/select_n | solution.py:521
  72.1 2.0 copy-done
  74.1 1.3 convolution_convert_fusion
  75.4 0.7 copy.13.down
  76.2 9.2 %collective-permute-done.6.two_a = bf16[1568,256]{1,0:T(8,128)(2,1)} collective-permute-done((bf16[1568,256]{1,0:T(8,128)(2,1)}, bf16[1568,256]{1,0:T(8,128)(2,1)}, u32[]{:S(2)}, u32[]{:S(2)}) %collective-permute-start.6) | collective-permute-done | bytes 802848 | tf_op jit(solution)/shard_map/ppermute | solution.py:494
  85.3 0.7 slice_bitcast_fusion.1
  86.0 0.6 pad_maximum_fusion.4.ups
  86.7 0.6 collective-permute-done.8.two_b
  87.3 6.3 %project_line.1.so_far = f32[256,1024]{1,0:T(8,128)} custom-call(bf16[256,8192]{1,0:T(8,128)(2,1)} %copy-done, bf16[8192,128]{1,0:T(8,128)(2,1)} %own_key.5, bf16[8192,128]{1,0:T(8,128)(2,1)} %own_val.5, bf16[3104,256]{1,0:T(8,128)(2,1)} %copy-done.3, bf16[1568,256]{1,0:T(8,128)(2,1)} %collective-permute-done.6.two_a, ...), custom_call_target="tpu_custom_call" | custom-call | flops 1610612736 | bytes 8388608 | tf_op jit(solution)/shard_map/project_line/pallas_call | solution.py:139
  93.5 4.3 %all-gather.3.cloned.1.call-done.far = bf16[5120,768]{1,0:T(8,128)(2,1)} async-done(((bf16[320,768]{1,0:T(8,128)(2,1)}), bf16[5120,768]{1,0:T(8,128)(2,1)}) %all-gather.3.cloned.1.call-update) | async-done | bytes 7864336 | tf_op jit(solution)/shard_map/all_gather | solution.py:505
  97.8 8.6 %project.1 = bf16[4,288,384]{2,1,0:T(8,128)(2,1)} custom-call(s32[2]{0:T(128)} %pad_add_fusion.place, bf16[256,8192]{1,0:T(8,128)(2,1)} %copy-done, bf16[8192,128]{1,0:T(8,128)(2,1)} %own_key.5, bf16[8192,128]{1,0:T(8,128)(2,1)} %own_val.5, bf16[5120,768]{1,0:T(8,128)(2,1)} %all-gather.3.cloned.1.call-done.far, f32[256,1024]{1,0:T(8,128)} %project_line.1.so_far, ...), custom_call_target="tpu_custom_call" | custom-call | flops 2684354560 | bytes 14680064 | tf_op jit(solution)/shard_map/project/pallas_call | solution.py:182
  106.4 0.0 copy-start.2
  106.4 4.7 %all-to-all-start = ((bf16[4,288,384]{2,1,0:T(8,128)(2,1)}), bf16[4,288,384]{2,1,0:T(8,128)(2,1)}, u32[]{:S(2)}, u32[]{:S(2)}) async-start(bf16[4,288,384]{2,1,0:T(8,128)(2,1)} %project.1), calls=%async_computation | async-start | bytes 1769472 | tf_op jit(solution)/shard_map/all_to_all | solution.py:534
  111.1 2.5 %pad_maximum_fusion = (f32[1024,128]{1,0:T(8,128)}, f32[1024,128]{1,0:T(8,128)}) fusion(f32[1024,64]{1,0:T(8,128)} %copy-done.9, f32[1024,64]{1,0:T(8,128)S(1)} %copy-done.6, f32[1024,64]{1,0:T(8,128)S(1)} %copy-done.8), kind=kLoop, calls=%fused_computation.14 | loop fusion | flops 262144 | bytes 1835008 | tf_op jit(solution)/shard_map/concatenate | solution.py:39
  113.7 2.3 %fusion.3 = f32[128]{0:T(128)S(1)} fusion(bf16[32,8192]{1,0:T(8,128)(2,1)} %factor.1, bf16[32,128]{1,0:T(8,128)(2,1)S(1)} %copy-done.15, bf16[8192,128]{1,0:T(8,128)(2,1)S(1)} %copy-done.2), kind=kOutput, calls=%fused_computation.6 | convolution fusion | flops 72351616 | bytes 2630144 | tf_op jit(solution)/shard_map/dot_general | solution.py:526
  116.0 0.5 sqrt_bitcast_fusion
  116.5 16.4 %all-to-all-done.rows = bf16[4,288,384]{2,1,0:T(8,128)(2,1)} async-done(((bf16[4,288,384]{2,1,0:T(8,128)(2,1)}), bf16[4,288,384]{2,1,0:T(8,128)(2,1)}, u32[]{:S(2)}, u32[]{:S(2)}) %all-to-all-start) | async-done | bytes 884768 | tf_op jit(solution)/shard_map/all_to_all | solution.py:534
  132.9 12.0 %attend.1 = (bf16[1024,256]{1,0:T(8,128)(2,1)}, f32[256,128]{1,0:T(8,128)}) custom-call(bf16[1024,512]{1,0:T(8,128)(2,1)} %query.1, bf16[1024,512]{1,0:T(8,128)(2,1)} %grad.1, bf16[4,288,384]{2,1,0:T(8,128)(2,1)} %all-to-all-done.rows, f32[1,128]{1,0:T(1,128)} %get-tuple-element.25.col_scale, f32[1,128]{1,0:T(1,128)} %get-tuple-element.24.norms, ...), custom_call_target="tpu_custom_call" | custom-call | flops 5368709120 | bytes 6291456 | tf_op jit(solution)/shard_map/attend/pallas_call | solution.py:276
  145.0 0.0 all-gather.5.cloned.1.call-update
  145.0 17.9 %all_to_all.21.grads = bf16[4,256,256]{2,1,0:T(8,128)(2,1)} all-to-all(bf16[4,256,256]{2,1,0:T(8,128)(2,1)} %bitcast.26), channel_id=1, replica_groups=mesh['x'=4,'y'=4,'zh'=2,'zl'=4,'core'=2] {'zl'}, dimensions={0} | all-to-all | bytes 1048576 | tf_op jit(solution)/shard_map/all_to_all | solution.py:536
  162.9 10.1 %back.1 = (bf16[128,8192]{1,0:T(8,128)(2,1)}, bf16[128,8192]{1,0:T(8,128)(2,1)}) custom-call(s32[2]{0:T(128)} %pad_add_fusion.place, bf16[4,256,256]{2,1,0:T(8,128)(2,1)} %all_to_all.21.grads, bf16[8192,128]{1,0:T(8,128)(2,1)} %own_key.5, bf16[8192,128]{1,0:T(8,128)(2,1)} %own_val.5, bf16[5120,768]{1,0:T(8,128)(2,1)} %all-gather.3.cloned.1.call-done.far, ...), custom_call_target="tpu_custom_call" | custom-call | tf_op jit(solution)/shard_map/back/pallas_call | solution.py:356
  173.1 1.8 collective-permute-start.10
  174.9 1.9 rank_part.1.part
  176.8 0.0 collective-permute-start.9
  176.8 2.3 %collective-permute-done.9.got = f32[256,32]{1,0:T(8,128)S(1)} collective-permute-done((f32[256,32]{1,0:T(8,128)}, f32[256,32]{1,0:T(8,128)S(1)}, u32[]{:S(2)}, u32[]{:S(2)}) %collective-permute-start.9) | collective-permute-done | bytes 32800 | tf_op jit(solution)/shard_map/ppermute | solution.py:539
  179.0 0.7 copy-done.14
  179.7 4.7 %down_part.1 = (bf16[1024,128]{1,0:T(8,128)(2,1)}, bf16[256,32]{1,0:T(8,128)(2,1)}) custom-call(s32[2]{0:T(128)} %pad_add_fusion.place, f32[256,32]{1,0:T(8,128)} %rank_part.1.part, f32[256,32]{1,0:T(8,128)} %copy-done.14, bf16[256,8192]{1,0:T(8,128)(2,1)} %copy-done), custom_call_target="tpu_custom_call" | custom-call | flops 134217728 | bytes 5242880 | tf_op jit(solution)/shard_map/down_part/pallas_call | solution.py:434
  184.4 12.0 %all-to-all-start.2 = ((bf16[128,8,128]{2,1,0:T(8,128)(2,1)}), bf16[128,8,128]{2,1,0:T(8,128)(2,1)S(1)}, u32[]{:S(2)}, u32[]{:S(2)}) async-start(bf16[128,8,128]{2,1,0:T(8,128)(2,1)} %bitcast.27), calls=%async_computation.2 | async-start | bytes 524288 | tf_op jit(solution)/shard_map/all_to_all | solution.py:543
  196.5 0.0 all-gather.5.cloned.1.call-done
  196.5 1.6 fold.1._.small
  198.1 4.5 %collective-permute-start.11 = (f32[40,128]{1,0:T(8,128)}, f32[40,128]{1,0:T(8,128)S(1)}, u32[]{:S(2)}, u32[]{:S(2)}) collective-permute-start(f32[40,128]{1,0:T(8,128)} %fold.1._.small), channel_id=1, source_target_pairs={{0,8},{8,0},{1,9},{9,1},{2,10},{10,2},{3,11},{11,3},{4,12},{12,4},... | collective-permute-start | bytes 61448 | tf_op jit(solution)/shard_map/ppermute | solution.py:545
  202.6 1.3 copy-done.10
  203.9 5.2 %join.1._ = bf16[128,8192]{1,0:T(8,128)(2,1)} custom-call(s32[2]{0:T(128)} %pad_add_fusion.place, bf16[256,32]{1,0:T(8,128)(2,1)} %get-tuple-element.14.rank, bf16[32,8192]{1,0:T(8,128)(2,1)} %factor.1, bf16[128,8192]{1,0:T(8,128)(2,1)} %get-tuple-element.16.mine, bf16[128,8192]{1,0:T(8,128)(2,1)} %copy-done.10, f32[40,128]{1,0:T(8,128)} %fold.1._.small), custom_call_target="tpu_custom_call" | custom-call | tf_op jit(solution)/shard_map/join/pallas_call | solution.py:401
  209.2 1.4 all-to-all-done.2
  210.6 0.7 copy-done.13
  211.3 0.0 copy-done.16
  211.3 1.8 finish.1
  213.1 1.2 slice_bitcast_fusion.3
  (43 shorter events, 0.1 us)
Async XLA Ops:
  7.2 18.1 %copy-start.1 = (bf16[8192,128]{1,0:T(8,128)(2,1)S(1)}, bf16[8192,128]{1,0:T(8,128)(2,1)}, u32[]{:S(2)}) copy-start(bf16[8192,128]{1,0:T(8,128)(2,1)} %own_key.5) | copy-start | bytes 6291460
  7.2 18.6 %slice-start = ((bf16[8192,128]{1,0:T(8,128)(2,1)}), bf16[3072,128]{1,0:T(8,128)(2,1)S(1)}, s32[]{:S(2)}) async-start(bf16[8192,128]{1,0:T(8,128)(2,1)} %own_key.5), calls=%async_computation.5 | async-start | bytes 1572864 | tf_op jit(solution)/shard_map/slice | solution.py:506
  7.2 18.6 %copy-start.15 = (bf16[32,128]{1,0:T(8,128)(2,1)S(1)}, bf16[32,128]{1,0:T(8,128)(2,1)}, u32[]{:S(2)}) copy-start(bf16[32,128]{1,0:T(8,128)(2,1)} %param.12) | copy-start | bytes 24580
  7.2 90.6 %all-gather.3.cloned.1.call-start = ((), (), s32[]{:S(2)}) async-start(), calls=%async_computation.3 | async-start | bytes 8355840 | tf_op jit(solution)/shard_map/all_gather | solution.py:505
  8.4 14.0 %collective-permute-start.4 = (bf16[320,256]{1,0:T(8,128)(2,1)S(1)}, bf16[320,256]{1,0:T(8,128)(2,1)S(1)}, u32[]{:S(2)}, u32[]{:S(2)}) collective-permute-start(bf16[320,256]{1,0:T(8,128)(2,1)S(1)} %pad_maximum_fusion.3), channel_id=1, source_target_pairs={{0,2},{2,4},{4,6},{6,8},{8,10},{10,12},{12,14},{14,0},{1,3},{3,5},... | collective-permute-start | bytes 491528 | tf_op jit(solution)/shard_map/ppermute | solution.py:494
  10.9 11.5 %collective-permute-start.1 = (bf16[320,256]{1,0:T(8,128)(2,1)S(1)}, bf16[320,256]{1,0:T(8,128)(2,1)S(1)}, u32[]{:S(2)}, u32[]{:S(2)}) collective-permute-start(bf16[320,256]{1,0:T(8,128)(2,1)S(1)} %pad_maximum_fusion.3), channel_id=1, source_target_pairs={{0,14},{2,0},{4,2},{6,4},{8,6},{10,8},{12,10},{14,12},{1,15},{3,1}... | collective-permute-start | bytes 491528 | tf_op jit(solution)/shard_map/ppermute | solution.py:494
  15.0 7.4 %collective-permute-start.3 = (bf16[160,256]{1,0:T(8,128)(2,1)S(1)}, bf16[160,256]{1,0:T(8,128)(2,1)S(1)}, u32[]{:S(2)}, u32[]{:S(2)}) collective-permute-start(bf16[160,256]{1,0:T(8,128)(2,1)S(1)} %get-tuple-element.23), channel_id=1, source_target_pairs={{0,4},{2,6},{4,8},{6,10},{8,12},{10,14},{12,0},{14,2},{1,5},{3,7},... | collective-permute-start | bytes 245768 | tf_op jit(solution)/shard_map/ppermute | solution.py:494
  15.1 7.3 %collective-permute-start.2 = (bf16[160,256]{1,0:T(8,128)(2,1)S(1)}, bf16[160,256]{1,0:T(8,128)(2,1)S(1)}, u32[]{:S(2)}, u32[]{:S(2)}) collective-permute-start(bf16[160,256]{1,0:T(8,128)(2,1)S(1)} %get-tuple-element.22), channel_id=1, source_target_pairs={{0,12},{2,14},{4,0},{6,2},{8,4},{10,6},{12,8},{14,10},{1,13},{3,15... | collective-permute-start | bytes 245768 | tf_op jit(solution)/shard_map/ppermute | solution.py:494
  23.3 2.5 %slice-start.1 = ((bf16[8192,128]{1,0:T(8,128)(2,1)}), bf16[3072,128]{1,0:T(8,128)(2,1)S(1)}, s32[]{:S(2)}) async-start(bf16[8192,128]{1,0:T(8,128)(2,1)} %own_val.5), calls=%async_computation.6 | async-start | bytes 1572864 | tf_op jit(solution)/shard_map/slice | solution.py:506
  23.3 45.5 %collective-permute-start = (bf16[128,8192]{1,0:T(8,128)(2,1)}, bf16[128,8192]{1,0:T(8,128)(2,1)}, u32[]{:S(2)}, u32[]{:S(2)}) collective-permute-start(bf16[128,8192]{1,0:T(8,128)(2,1)} %param.8), channel_id=1, source_target_pairs={{0,1},{1,0},{2,3},{3,2},{4,5},{5,4},{6,7},{7,6},{8,9},{9,8},{10,11... | collective-permute-start | bytes 6291464 | tf_op jit(solution)/shard_map/ppermute | solution.py:520
  27.9 36.0 %collective-permute-start.5 = (bf16[3104,256]{1,0:T(8,128)(2,1)}, bf16[3104,256]{1,0:T(8,128)(2,1)S(1)}, u32[]{:S(2)}, u32[]{:S(2)}) collective-permute-start(bf16[3104,256]{1,0:T(8,128)(2,1)} %fusion.5), channel_id=1, source_target_pairs={{0,14},{2,0},{4,2},{6,4},{8,6},{10,8},{12,10},{14,12},{1,15},{3,1}... | collective-permute-start | bytes 4767752 | tf_op jit(solution)/shard_map/ppermute | solution.py:494
  29.0 38.3 %collective-permute-start.7 = (bf16[3104,256]{1,0:T(8,128)(2,1)}, bf16[3104,256]{1,0:T(8,128)(2,1)S(1)}, u32[]{:S(2)}, u32[]{:S(2)}) collective-permute-start(bf16[3104,256]{1,0:T(8,128)(2,1)} %fusion.5), channel_id=1, source_target_pairs={{0,2},{2,4},{4,6},{6,8},{8,10},{10,12},{12,14},{14,0},{1,3},{3,5},... | collective-permute-start | bytes 4767752 | tf_op jit(solution)/shard_map/ppermute | solution.py:494
  29.9 38.8 %copy-start.12 = (bf16[128,8192]{1,0:T(8,128)(2,1)S(1)}, bf16[128,8192]{1,0:T(8,128)(2,1)}, u32[]{:S(2)}) copy-start(bf16[128,8192]{1,0:T(8,128)(2,1)} %param.8) | copy-start | bytes 6291460
  31.9 0.8 copy-start.5
  31.9 1.6 copy-start.7
  31.9 1.6 copy-start.9
  63.9 8.2 %copy-start.3 = (bf16[3104,256]{1,0:T(8,128)(2,1)}, bf16[3104,256]{1,0:T(8,128)(2,1)S(1)}, u32[]{:S(2)}) copy-start(bf16[3104,256]{1,0:T(8,128)(2,1)S(1)} %collective-permute-done.5.one) | copy-start | bytes 4767748
  64.9 20.4 %collective-permute-start.6 = (bf16[1568,256]{1,0:T(8,128)(2,1)}, bf16[1568,256]{1,0:T(8,128)(2,1)}, u32[]{:S(2)}, u32[]{:S(2)}) collective-permute-start(bf16[1568,256]{1,0:T(8,128)(2,1)} %slice.48), channel_id=1, source_target_pairs={{0,14},{2,0},{4,2},{6,4},{8,6},{10,8},{12,10},{14,12},{1,15},{3,1}... | collective-permute-start | bytes 2408456 | tf_op jit(solution)/shard_map/ppermute | solution.py:494
  67.3 4.8 %copy-start.4 = (bf16[3104,256]{1,0:T(8,128)(2,1)}, bf16[3104,256]{1,0:T(8,128)(2,1)S(1)}, u32[]{:S(2)}) copy-start(bf16[3104,256]{1,0:T(8,128)(2,1)S(1)} %collective-permute-done.7.three) | copy-start | bytes 4767748
  68.3 18.9 %collective-permute-start.8 = (bf16[1536,256]{1,0:T(8,128)(2,1)}, bf16[1536,256]{1,0:T(8,128)(2,1)}, u32[]{:S(2)}, u32[]{:S(2)}) collective-permute-start(bf16[1536,256]{1,0:T(8,128)(2,1)} %slice.49), channel_id=1, source_target_pairs={{0,2},{2,4},{4,6},{6,8},{8,10},{10,12},{12,14},{14,0},{1,3},{3,5},... | collective-permute-start | bytes 2359304 | tf_op jit(solution)/shard_map/ppermute | solution.py:494
  68.8 5.3 %copy-start.11 = (bf16[32,8192]{1,0:T(8,128)(2,1)S(1)}, bf16[32,8192]{1,0:T(8,128)(2,1)}, u32[]{:S(2)}) copy-start(bf16[32,8192]{1,0:T(8,128)(2,1)} %factor.1) | copy-start | bytes 1572868
  72.1 2.0 copy-start
  97.8 13.3 %copy-start.6 = (f32[1024,64]{1,0:T(8,128)S(1)}, f32[1024,64]{1,0:T(8,128)}, u32[]{:S(2)}) copy-start(f32[1024,64]{1,0:T(8,128)} %copy-done.5) | copy-start | bytes 786436
  97.8 13.3 %copy-start.8 = (f32[1024,64]{1,0:T(8,128)S(1)}, f32[1024,64]{1,0:T(8,128)}, u32[]{:S(2)}) copy-start(f32[1024,64]{1,0:T(8,128)} %copy-done.7) | copy-start | bytes 786436
  106.4 7.2 %copy-start.2 = (bf16[8192,128]{1,0:T(8,128)(2,1)S(1)}, bf16[8192,128]{1,0:T(8,128)(2,1)}, u32[]{:S(2)}) copy-start(bf16[8192,128]{1,0:T(8,128)(2,1)} %own_val.5) | copy-start | bytes 6291460
  106.4 26.5 %all-to-all-start = ((bf16[4,288,384]{2,1,0:T(8,128)(2,1)}), bf16[4,288,384]{2,1,0:T(8,128)(2,1)}, u32[]{:S(2)}, u32[]{:S(2)}) async-start(bf16[4,288,384]{2,1,0:T(8,128)(2,1)} %project.1), calls=%async_computation | async-start | bytes 1769472 | tf_op jit(solution)/shard_map/all_to_all | solution.py:534
  111.1 85.4 %all-gather.5.cloned.1.call-start = ((), (), s32[]{:S(2)}) async-start(), calls=%async_computation.4 | async-start | bytes 2228224 | tf_op jit(solution)/shard_map/all_gather | solution.py:537
  113.6 2.3 %copy-start.17 = (f32[128]{0:T(128)S(1)}, f32[128]{0:T(128)}, u32[]{:S(2)}) copy-start(f32[128]{0:T(128)} %param.13) | copy-start | bytes 1540
  173.1 29.5 %collective-permute-start.10 = (bf16[128,8192]{1,0:T(8,128)(2,1)}, bf16[128,8192]{1,0:T(8,128)(2,1)S(1)}, u32[]{:S(2)}, u32[]{:S(2)}) collective-permute-start(bf16[128,8192]{1,0:T(8,128)(2,1)} %get-tuple-element.17), channel_id=1, source_target_pairs={{0,1},{1,0},{2,3},{3,2},{4,5},{5,4},{6,7},{7,6},{8,9},{9,8},{10,11... | collective-permute-start | bytes 6291464 | tf_op jit(solution)/shard_map/ppermute | solution.py:541
  176.8 2.3 %collective-permute-start.9 = (f32[256,32]{1,0:T(8,128)}, f32[256,32]{1,0:T(8,128)S(1)}, u32[]{:S(2)}, u32[]{:S(2)}) collective-permute-start(f32[256,32]{1,0:T(8,128)} %rank_part.1.part), channel_id=1, source_target_pairs={{0,1},{1,0},{2,3},{3,2},{4,5},{5,4},{6,7},{7,6},{8,9},{9,8},{10,11... | collective-permute-start | bytes 98312 | tf_op jit(solution)/shard_map/ppermute | solution.py:539
  179.0 0.7 copy-start.14
  184.4 26.1 %all-to-all-start.2 = ((bf16[128,8,128]{2,1,0:T(8,128)(2,1)}), bf16[128,8,128]{2,1,0:T(8,128)(2,1)S(1)}, u32[]{:S(2)}, u32[]{:S(2)}) async-start(bf16[128,8,128]{2,1,0:T(8,128)(2,1)} %bitcast.27), calls=%async_computation.2 | async-start | bytes 524288 | tf_op jit(solution)/shard_map/all_to_all | solution.py:543
  198.1 12.5 %collective-permute-start.11 = (f32[40,128]{1,0:T(8,128)}, f32[40,128]{1,0:T(8,128)S(1)}, u32[]{:S(2)}, u32[]{:S(2)}) collective-permute-start(f32[40,128]{1,0:T(8,128)} %fold.1._.small), channel_id=1, source_target_pairs={{0,8},{8,0},{1,9},{9,1},{2,10},{10,2},{3,11},{11,3},{4,12},{12,4},... | collective-permute-start | bytes 61448 | tf_op jit(solution)/shard_map/ppermute | solution.py:545
  202.6 1.3 copy-start.10
  210.6 0.7 copy-start.13
  210.6 0.7 copy-start.16
Sparse Core Ops, SparseCore 0:
  23.4 74.3 all-gather.2
  145.1 49.2 all-gather.4

commit v2 on v1

--- a/solution.py
+++ b/solution.py
@@ -53,6 +53,10 @@
 
 def cost(flops, moved, trans=0):
     return pl.CostEstimate(flops=flops, bytes_accessed=moved, transcendentals=trans)
+
+
+def in_vmem():
+    return pl.BlockSpec(memory_space=pltpu.VMEM)
 
 
 def any_ref():
@@ -299,28 +303,8 @@
     )(queries, grad_attn, rows, col_scale, norms, cos, sin)
 
 
-def rank_kernel(place, grads, ups, out):
-    total = jnp.zeros((PAIR, RANK), F32)
-    for r in range(4):
-        slot = lax.rem(place[0] + r, 4)
-        total += lax.dot_general(grads[slot, :, HD:], ups[r], NT, preferred_element_type=F32)
-    out[...] = total
-
-
-def rank_part(place, grads, ups):
-    return pl.pallas_call(
-        rank_kernel,
-        in_specs=[smem(), whole((4, PAIR, 2 * HD)), whole((4, RANK, HD))],
-        out_specs=whole((PAIR, RANK)),
-        out_shape=jax.ShapeDtypeStruct((PAIR, RANK), F32),
-        compiler_params=params(60),
-        cost_estimate=cost(2 * PAIR * 512 * RANK, MIB),
-        name="rank_part",
-    )(place, grads, ups)
-
-
 def back_kernel(
-    place, grads, own_key, own_val, far, one, two_a, two_b, three, _, mine, theirs,
+    place, grads, ups, own_key, own_val, far, one, two_a, two_b, three, _, mine, theirs, rank,
     left, weights, part, far_sems, line_sems, out_sem,
 ):
     chunks = near_copies(0, 0, own_key, own_val, far, weights, far_sems)
@@ -333,6 +317,9 @@
         slot = lax.rem(place[0] + r, 4)
         left[:128, r * 256 : (r + 1) * 256] = grads[slot, pl.ds(first, 128), :]
         left[128:, r * 256 : (r + 1) * 256] = grads[slot, pl.ds(second, 128), :]
+        term = lax.dot_general(grads[slot, :, HD:], ups[r], NT, preferred_element_type=F32)
+        total = term if r == 0 else total + term
+    rank[...] = total
     leaving = []
     base = 0
     for i, chunk in enumerate(chunks):
@@ -351,13 +338,13 @@
     wait_all(leaving)
 
 
-def back(place, grads, w_key, w_val, far, line, after):
+def back(place, grads, ups, w_key, w_val, far, line, after):
     count = NEAR // CHUNK
     return pl.pallas_call(
         back_kernel,
-        in_specs=[smem(), whole((4, PAIR, 2 * HD))] + [any_ref()] * 8,
-        out_specs=[any_ref()] * 2,
-        out_shape=[jax.ShapeDtypeStruct((128, D), BF)] * 2,
+        in_specs=[smem(), in_vmem(), in_vmem()] + [any_ref()] * 8,
+        out_specs=[any_ref(), any_ref(), in_vmem()],
+        out_shape=[jax.ShapeDtypeStruct((128, D), BF)] * 2 + [jax.ShapeDtypeStruct((PAIR, RANK), F32)],
         scratch_shapes=[
             pltpu.VMEM((PAIR, 1024), BF),
             pltpu.VMEM((D, 1024), BF),
@@ -369,29 +356,23 @@
         compiler_params=params(60),
         cost_estimate=cost(0, 0),
         name="back",
-    )(place, grads, w_key, w_val, far, *line, after)
-
-
-def join_kernel(place, rank, factor, mine, theirs, _, out, one, two, result, sems, out_sem):
+    )(place, grads, ups, w_key, w_val, far, *line, after)
+
+
+def join_kernel(place, rank, factor, mine, theirs, _, out, mark, one, result, sems, out_sem):
+    mark[...] = jnp.zeros_like(mark)
     size = D // 8
     chunks = []
     for i in range(8):
         cols = pl.ds(i * size, size)
-        chunks.append(
-            start_all(
-                [
-                    pltpu.make_async_copy(mine.at[:, cols], one.at[:, cols], sems.at[0, i]),
-                    pltpu.make_async_copy(theirs.at[:, cols], two.at[:, cols], sems.at[1, i]),
-                ]
-            )
-        )
+        chunks.append(start_all([pltpu.make_async_copy(mine.at[:, cols], one.at[:, cols], sems.at[i])]))
     own = rank[pl.ds(pl.multiple_of(place[1] * 128, 128), 128), :]
     leaving = []
     for i, chunk in enumerate(chunks):
         here = slice(i * size, (i + 1) * size)
         adapter = SCALE * jnp.dot(own, factor[:, here], preferred_element_type=F32)
         wait_all(chunk)
-        result[:, here] = (one[:, here].astype(F32) + two[:, here].astype(F32) + adapter).astype(BF)
+        result[:, here] = (one[:, here].astype(F32) + theirs[:, here].astype(F32) + adapter).astype(BF)
         cols = pl.ds(i * size, size)
         leaving += start_all([pltpu.make_async_copy(result.at[:, cols], out.at[:, cols], out_sem.at[i])])
     wait_all(leaving)
@@ -400,49 +381,48 @@
 def join(place, rank, factor, mine, theirs, after):
     return pl.pallas_call(
         join_kernel,
-        in_specs=[smem(), whole((PAIR, RANK)), whole((RANK, D))] + [any_ref()] * 3,
-        out_specs=any_ref(),
-        out_shape=jax.ShapeDtypeStruct((128, D), BF),
-        scratch_shapes=[pltpu.VMEM((128, D), BF)] * 3
-        + [pltpu.SemaphoreType.DMA((2, 8)), pltpu.SemaphoreType.DMA((8,))],
-        compiler_params=params(60),
+        in_specs=[smem(), in_vmem(), whole((RANK, D)), any_ref(), in_vmem(), any_ref()],
+        out_specs=[any_ref(), in_vmem()],
+        out_shape=[jax.ShapeDtypeStruct((128, D), BF), jax.ShapeDtypeStruct((8, HD), F32)],
+        scratch_shapes=[pltpu.VMEM((128, D), BF)] * 2 + [pltpu.SemaphoreType.DMA((8,))] * 2,
+        compiler_params=params(16),
         cost_estimate=cost(0, 0),
         name="join",
     )(place, rank, factor, mine, theirs, after)
 
 
-def down_kernel(place, part, got, hid, out, rank):
+def down_kernel(place, part, got, pair, out, rank, hid, sems):
+    chunks = [start_all([copy]) for copy in pair_copies(pair, hid, 0, 4, sems)]
     rank[...] = (part[...] + got[...]).astype(BF)
-    product = SCALE * lax.dot_general(rank[...], hid[...], TN, preferred_element_type=F32)
     lane = lax.broadcasted_iota(jnp.int32, (8, HD), 1) // 32
     core = place[1]
-    for tile in range(product.shape[1] // HD):
-        regs = [product[8 * i : 8 * i + 8, tile * HD : (tile + 1) * HD] for i in range(4)]
-        blocks = []
-        for pick in range(2):
-            column = 2 * pick + core
-            block = jnp.zeros((8, HD), F32)
-            for i in range(4):
-                moved = pltpu.roll(regs[i], lax.rem((i - column + 4) * 32, HD), 1)
-                block = jnp.where(lane == i, moved, block)
-            blocks.append(block)
-        out[16 * tile : 16 * tile + 16, :] = jnp.concatenate(blocks, axis=0).astype(BF)
+    size = D // 4
+    for step, chunk in enumerate(chunks):
+        wait_all(chunk)
+        here = hid[:, step * size : (step + 1) * size]
+        product = SCALE * lax.dot_general(rank[...], here, TN, preferred_element_type=F32)
+        for tile in range(size // HD):
+            regs = [product[8 * i : 8 * i + 8, tile * HD : (tile + 1) * HD] for i in range(4)]
+            blocks = []
+            for pick in range(2):
+                column = 2 * pick + core
+                block = jnp.zeros((8, HD), F32)
+                for i in range(4):
+                    moved = pltpu.roll(regs[i], lax.rem((i - column + 4) * 32, HD), 1)
+                    block = jnp.where(lane == i, moved, block)
+                blocks.append(block)
+            first = step * (size // 8) + 16 * tile
+            out[first : first + 16, :] = jnp.concatenate(blocks, axis=0).astype(BF)
 
 
 def down_part(place, part, got, pair):
-    wide = 2048
     return pl.pallas_call(
         down_kernel,
-        grid=(D // wide,),
-        in_specs=[
-            smem(),
-            whole((PAIR, RANK)),
-            whole((PAIR, RANK)),
-            pl.BlockSpec((PAIR, wide), lambda k: (0, k)),
-        ],
-        out_specs=[pl.BlockSpec((wide // 8, HD), lambda k: (k, 0)), whole((PAIR, RANK))],
+        in_specs=[smem(), in_vmem(), in_vmem(), any_ref()],
+        out_specs=[whole((1024, HD)), in_vmem()],
         out_shape=[jax.ShapeDtypeStruct((1024, HD), BF), jax.ShapeDtypeStruct((PAIR, RANK), BF)],
-        compiler_params=params(60),
+        scratch_shapes=[pltpu.VMEM((PAIR, D), BF), pltpu.SemaphoreType.DMA((4,))],
+        compiler_params=params(58),
         cost_estimate=cost(2 * PAIR * D * RANK, 5 * MIB),
         name="down_part",
     )(place, part, got, pair)
@@ -471,20 +451,20 @@
         out[8 * i : 8 * i + 8, :] = total[:, 32 * i : 32 * i + 32]
     sums = small[...] + other[...]
     up_grad[...] = sums[:RANK]
-    mag_grad[...] = sums[RANK:]
+    mag_grad[...] = sums[RANK : RANK + 1]
 
 
 def finish(pieces, small, other, after):
     return pl.pallas_call(
         finish_kernel,
-        in_specs=[whole((1024, HD)), whole((40, HD)), whole((40, HD)), any_ref()],
-        out_specs=[whole((RANK, 32)), whole((RANK, HD)), whole((8, HD))],
+        in_specs=[in_vmem(), in_vmem(), in_vmem(), any_ref()],
+        out_specs=[whole((RANK, 32)), whole((RANK, HD)), whole((1, HD))],
         out_shape=[
             jax.ShapeDtypeStruct((RANK, 32), F32),
             jax.ShapeDtypeStruct((RANK, HD), F32),
-            jax.ShapeDtypeStruct((8, HD), F32),
-        ],
-        compiler_params=params(60),
+            jax.ShapeDtypeStruct((1, HD), F32),
+        ],
+        compiler_params=params(8),
         cost_estimate=cost(0, 0),
         name="finish",
     )(pieces, small, other, after)
@@ -535,17 +515,16 @@
     grads, small = attend(queries, grad_attn, rows, col_scale, norms.reshape(1, HD), cos, sin)
     grads = lax.all_to_all(grads.reshape(4, PAIR, 2 * HD), "zl", 0, 0, tiled=True)
     gathered = lax.all_gather(small, ("x", "y"), axis=0, tiled=True)
-    part = rank_part(place, grads, ups)
+    mine, theirs, part = back(place, grads, ups, w_key, w_val, far, line, small)
     got = lax.ppermute(part, "core", swap)
-    mine, theirs = back(place, grads, w_key, w_val, far, line, small)
     theirs = lax.ppermute(theirs, "core", swap)
     pieces, rank = down_part(place, part, got, pair)
     pieces = lax.all_to_all(pieces, DP + ("zl",), 0, 0, tiled=True)
     small = fold(gathered.reshape(16, SMALL, HD))
     other = lax.ppermute(small, "zh", swap)
-    grad_hidden = join(place, rank, factor, mine, theirs, small)
-    grad_down, up_sum, mag_sum = finish(pieces, small, other, grad_hidden)
-    return grad_hidden, grad_down, up_sum, mag_sum[0]
+    grad_hidden, mark = join(place, rank, factor, mine, theirs, small)
+    grad_down, up_sum, mag_sum = finish(pieces, small, other, mark)
+    return grad_hidden, grad_down, up_sum, mag_sum.reshape(HD)
 
 
 def solution(mesh):

time: 222 us -> 219 us (0.986)
  Pallas kernels: 52.3 us -> 49.5 us
    all_gather x1, waiting for transfers between devices: 4.26 us -> 0.59 us  [gather_weights(): lax.all_gather(jnp.concatenate([first, second, third], axis=1), ('x', 'y'...]
    ppermute x8, waiting for transfers between devices: 43.9 us -> 46.4 us  [along_z(): lax.ppermute(value, ('zh', 'zl'), [(i, (i + shift) % 8) for i in range(8)])]
    pallas_call x5 -> x4, Pallas kernels: 23.7 us -> 21.2 us  [the longest x1 10.9 us: back(): pl.pallas_call(back_kernel, in_specs=[smem(), in_vmem(), in_vmem()] + [an...]
    unnamed x36 -> x30, local copies, waits for them, and re-layouts: 5.51 us -> 5.02 us
  transfers between devices with their start and end apart: 16 -> 16, of which waited for: 8 -> 9; matrix products, arithmetic and copies ran while one was open for 9% -> 10% of each run, Pallas kernels for 13% -> 13%
where the time goes in v2:
time: 219 us; the launch traced here: 218 us
  waiting for transfers between devices  69.5 us (32%)
  Pallas kernels  49.5 us (23%)
  starting transfers between devices  38.5 us (18%)
  blocking collectives  18 us (8%)
  other arithmetic  14.5 us (7%)
  between operations  14.2 us (6%)
  local copies, waits for them, and re-layouts  11.4 us (5%)
  matrix products  2.65 us (1%)
    ppermute x8, waiting for transfers between devices, along_z(): lax.ppermute(value, ('zh', 'zl'), [(i, (i + shift) % 8) for i in range(8)])  46.4 us
    all_to_all x1, blocking collectives, shards(): lax.all_to_all(grads.reshape(4, PAIR, 2 * HD), 'zl', 0, 0, tiled=True)  18 us
    all_to_all x1, waiting for transfers between devices, shards(): rows = lax.all_to_all(rows, 'zl', 0, 0, tiled=True)  17.3 us
    ppermute x8, starting transfers between devices, along_z(): lax.ppermute(value, ('zh', 'zl'), [(i, (i + shift) % 8) for i in range(8)])  12.7 us
    pallas_call x1, Pallas kernels, attend(): pl.pallas_call(attend_kernel, grid=(GROUP // HEADS,), in_specs=[pl.BlockS...  12 us
    all_to_all x1, starting transfers between devices, shards(): pieces = lax.all_to_all(pieces, DP + ('zl',), 0, 0, tiled=True)  12 us
    pallas_call x1, Pallas kernels, back(): pl.pallas_call(back_kernel, in_specs=[smem(), in_vmem(), in_vmem()] + [an...  10.9 us
    pallas_call x1, Pallas kernels, project(): pl.pallas_call(project_kernel, in_specs=[smem(), any_ref(), any_ref(), an...  8.54 us
  transfers between devices with their start and end apart: 16, of which 9 were waited for; matrix products, arithmetic and copies ran while one was open for 10% of the time, Pallas kernels for 13%

profile of v2, /device:TPU:1, one launch (start us, length us, event | category | flops | bytes accessed | tf_op | source)
XLA Modules:
  0.0 218.4 jit_solution(5911263687328821445)
XLA Ops:
  7.2 0.0 slice-start.1
  7.2 0.0 slice-start
  7.2 0.0 all-gather.3.cloned.1.call-start
  7.3 1.0 constant_dynamic-slice_fusion.1
  8.3 6.5 %collective-permute-start.1 = (bf16[320,256]{1,0:T(8,128)(2,1)S(1)}, bf16[320,256]{1,0:T(8,128)(2,1)S(1)}, u32[]{:S(2)}, u32[]{:S(2)}) collective-permute-start(bf16[320,256]{1,0:T(8,128)(2,1)S(1)} %pad_maximum_fusion.3), channel_id=1, source_target_pairs={{0,14},{2,0},{4,2},{6,4},{8,6},{10,8},{12,10},{14,12},{1,15},{3,1}... | collective-permute-start | bytes 491528 | tf_op jit(solution)/shard_map/ppermute | solution.py:474
  14.8 2.0 collective-permute-start.2
  16.8 0.5 collective-permute-start.3
  17.3 4.3 %collective-permute-done.2 = bf16[160,256]{1,0:T(8,128)(2,1)S(1)} collective-permute-done((bf16[160,256]{1,0:T(8,128)(2,1)S(1)}, bf16[160,256]{1,0:T(8,128)(2,1)S(1)}, u32[]{:S(2)}, u32[]{:S(2)}) %collective-permute-start.2) | collective-permute-done | bytes 81952 | tf_op jit(solution)/shard_map/ppermute | solution.py:474
  21.6 1.0 collective-permute-done.3
  22.6 0.0 collective-permute-done.1
  22.6 0.0 collective-permute-done.4
  22.6 0.8 pad_maximum_fusion.2
  23.4 0.0 all-gather.3.cloned.1.call-update
  23.4 2.5 %collective-permute-start = (bf16[128,8192]{1,0:T(8,128)(2,1)}, bf16[128,8192]{1,0:T(8,128)(2,1)}, u32[]{:S(2)}, u32[]{:S(2)}) collective-permute-start(bf16[128,8192]{1,0:T(8,128)(2,1)} %param.8), channel_id=1, source_target_pairs={{0,1},{1,0},{2,3},{3,2},{4,5},{5,4},{6,7},{7,6},{8,9},{9,8},{10,11... | collective-permute-start | bytes 6291464 | tf_op jit(solution)/shard_map/ppermute | solution.py:500
  26.0 1.2 fusion.13
  27.2 2.1 fusion.5
  29.2 1.1 collective-permute-start.5
  30.4 1.2 collective-permute-start.7
  31.5 0.6 pad_add_fusion.place
  32.1 2.0 fusion.6
  34.1 0.8 copy-done.9
  34.9 0.8 fusion.9
  35.7 31.2 %collective-permute-done.5.one = bf16[3104,256]{1,0:T(8,128)(2,1)S(1)} collective-permute-done((bf16[3104,256]{1,0:T(8,128)(2,1)}, bf16[3104,256]{1,0:T(8,128)(2,1)S(1)}, u32[]{:S(2)}, u32[]{:S(2)}) %collective-permute-start.5) | collective-permute-done | bytes 1589280 | tf_op jit(solution)/shard_map/ppermute | solution.py:474
  66.9 1.1 slice.44
  68.0 1.2 collective-permute-start.6
  69.2 0.0 collective-permute-done.7.three
  69.2 2.1 slice.45
  71.3 0.2 collective-permute-start.8
  71.5 0.7 slice_bitcast_fusion
  72.3 3.2 %maximum_select_fusion.pair = bf16[256,8192]{1,0:T(8,128)(2,1)S(1)} fusion(bf16[128,8192]{1,0:T(8,128)(2,1)} %collective-permute-done, bf16[128,8192]{1,0:T(8,128)(2,1)S(1)} %copy-done.11, pred[]{:T(512)S(6)} %eq.3), kind=kLoop, calls=%fused_computation.3 | loop fusion | flops 18874368 | bytes 8388609 | tf_op jit(solution)/shard_map/jit(_where)/select_n | solution.py:501
  75.5 2.0 copy-done.6
  77.5 1.4 convolution_convert_fusion
  78.8 0.7 copy.13.down
  79.6 7.7 %collective-permute-done.6.two_a = bf16[1568,256]{1,0:T(8,128)(2,1)} collective-permute-done((bf16[1568,256]{1,0:T(8,128)(2,1)}, bf16[1568,256]{1,0:T(8,128)(2,1)}, u32[]{:S(2)}, u32[]{:S(2)}) %collective-permute-start.6) | collective-permute-done | bytes 802848 | tf_op jit(solution)/shard_map/ppermute | solution.py:474
  87.3 0.7 slice_bitcast_fusion.1
  88.0 0.6 pad_maximum_fusion.4.ups
  88.6 2.2 %collective-permute-done.8.two_b = bf16[1536,256]{1,0:T(8,128)(2,1)} collective-permute-done((bf16[1536,256]{1,0:T(8,128)(2,1)}, bf16[1536,256]{1,0:T(8,128)(2,1)}, u32[]{:S(2)}, u32[]{:S(2)}) %collective-permute-start.8) | collective-permute-done | bytes 786464 | tf_op jit(solution)/shard_map/ppermute | solution.py:474
  90.8 6.1 %project_line.1.so_far = f32[256,1024]{1,0:T(8,128)} custom-call(bf16[256,8192]{1,0:T(8,128)(2,1)} %copy-done.6, bf16[8192,128]{1,0:T(8,128)(2,1)} %own_key.5, bf16[8192,128]{1,0:T(8,128)(2,1)} %own_val.5, bf16[3104,256]{1,0:T(8,128)(2,1)} %copy-done.8, bf16[1568,256]{1,0:T(8,128)(2,1)} %collective-permute-done.6.two_a, ...), custom_call_target="tpu_custom_call" | custom-call | flops 1610612736 | bytes 8388608 | tf_op jit(solution)/shard_map/project_line/pallas_call | solution.py:143
  96.9 0.6 all-gather.3.cloned.1.call-done.far
  97.5 8.5 %project.1 = bf16[4,288,384]{2,1,0:T(8,128)(2,1)} custom-call(s32[2]{0:T(128)} %pad_add_fusion.place, bf16[256,8192]{1,0:T(8,128)(2,1)} %copy-done.6, bf16[8192,128]{1,0:T(8,128)(2,1)} %own_key.5, bf16[8192,128]{1,0:T(8,128)(2,1)} %own_val.5, bf16[5120,768]{1,0:T(8,128)(2,1)} %all-gather.3.cloned.1.call-done.far, f32[256,1024]{1,0:T(8,128)} %project_line.1.so_far, ...), custom_call_target="tpu_custom_call" | custom-call | flops 2684354560 | bytes 14680064 | tf_op jit(solution)/shard_map/project/pallas_call | solution.py:186
  106.1 0.0 copy-start.7
  106.1 4.7 %all-to-all-start = ((bf16[4,288,384]{2,1,0:T(8,128)(2,1)}), bf16[4,288,384]{2,1,0:T(8,128)(2,1)}, u32[]{:S(2)}, u32[]{:S(2)}) async-start(bf16[4,288,384]{2,1,0:T(8,128)(2,1)} %project.1), calls=%async_computation | async-start | bytes 1769472 | tf_op jit(solution)/shard_map/all_to_all | solution.py:514
  110.7 2.7 %pad_maximum_fusion = (f32[1024,128]{1,0:T(8,128)}, f32[1024,128]{1,0:T(8,128)}) fusion(f32[1024,64]{1,0:T(8,128)} %copy-done.10, f32[1024,64]{1,0:T(8,128)S(1)} %get-tuple-element.32, f32[1024,64]{1,0:T(8,128)} %copy-done.9), kind=kLoop, calls=%fused_computation.14 | loop fusion | flops 262144 | bytes 1835008 | tf_op jit(solution)/shard_map/concatenate | solution.py:39
  113.4 1.3 fusion.3
  114.7 0.5 sqrt_bitcast_fusion
  115.2 17.3 %all-to-all-done.rows = bf16[4,288,384]{2,1,0:T(8,128)(2,1)} async-done(((bf16[4,288,384]{2,1,0:T(8,128)(2,1)}), bf16[4,288,384]{2,1,0:T(8,128)(2,1)}, u32[]{:S(2)}, u32[]{:S(2)}) %all-to-all-start) | async-done | bytes 884768 | tf_op jit(solution)/shard_map/all_to_all | solution.py:514
  132.6 12.0 %attend.1 = (bf16[1024,256]{1,0:T(8,128)(2,1)}, f32[256,128]{1,0:T(8,128)}) custom-call(bf16[1024,512]{1,0:T(8,128)(2,1)} %query.1, bf16[1024,512]{1,0:T(8,128)(2,1)} %grad.1, bf16[4,288,384]{2,1,0:T(8,128)(2,1)} %all-to-all-done.rows, f32[1,128]{1,0:T(1,128)} %get-tuple-element.31.col_scale, f32[1,128]{1,0:T(1,128)} %get-tuple-element.30.norms, ...), custom_call_target="tpu_custom_call" | custom-call | flops 5368709120 | bytes 6291456 | tf_op jit(solution)/shard_map/attend/pallas_call | solution.py:280
  144.6 0.0 all-gather.5.cloned.1.call-update
  144.6 18.0 %all_to_all.21.grads = bf16[4,256,256]{2,1,0:T(8,128)(2,1)} all-to-all(bf16[4,256,256]{2,1,0:T(8,128)(2,1)} %bitcast.25), channel_id=1, replica_groups=mesh['x'=4,'y'=4,'zh'=2,'zl'=4,'core'=2] {'zl'}, dimensions={0} | all-to-all | bytes 1048576 | tf_op jit(solution)/shard_map/all_to_all | solution.py:516
  162.6 10.9 %back.1 = (bf16[128,8192]{1,0:T(8,128)(2,1)}, bf16[128,8192]{1,0:T(8,128)(2,1)}, f32[256,32]{1,0:T(8,128)}) custom-call(s32[2]{0:T(128)} %pad_add_fusion.place, bf16[4,256,256]{2,1,0:T(8,128)(2,1)} %all_to_all.21.grads, bf16[4,32,128]{2,1,0:T(8,128)(2,1)} %pad_maximum_fusion.4.ups, bf16[8192,128]{1,0:T(8,128)(2,1)} %own_key.5, bf16[8192,128]{1,0:T(8,128)(2,1)} %own_val.5, ...), custom_call_target="tpu_custom_call" | custom-call | tf_op jit(solution)/shard_map/back/pallas_call | solution.py:343
  173.5 1.8 collective-permute-start.10
  175.3 0.4 collective-permute-start.9
  175.7 3.8 %collective-permute-done.9.got = f32[256,32]{1,0:T(8,128)S(1)} collective-permute-done((f32[256,32]{1,0:T(8,128)}, f32[256,32]{1,0:T(8,128)S(1)}, u32[]{:S(2)}, u32[]{:S(2)}) %collective-permute-start.9) | collective-permute-done | bytes 32800 | tf_op jit(solution)/shard_map/ppermute | solution.py:519
  179.5 0.6 copy-done.12
  180.1 4.5 %down_part.1 = (bf16[1024,128]{1,0:T(8,128)(2,1)}, bf16[256,32]{1,0:T(8,128)(2,1)}) custom-call(s32[2]{0:T(128)} %pad_add_fusion.place, f32[256,32]{1,0:T(8,128)} %get-tuple-element.18.part, f32[256,32]{1,0:T(8,128)} %copy-done.12, bf16[256,8192]{1,0:T(8,128)(2,1)} %copy-done.6), custom_call_target="tpu_custom_call" | custom-call | flops 134217728 | bytes 5242880 | tf_op jit(solution)/shard_map/down_part/pallas_call | solution.py:419
  184.7 12.0 %all-to-all-start.2 = ((bf16[128,8,128]{2,1,0:T(8,128)(2,1)}), bf16[128,8,128]{2,1,0:T(8,128)(2,1)S(1)}, u32[]{:S(2)}, u32[]{:S(2)}) async-start(bf16[128,8,128]{2,1,0:T(8,128)(2,1)} %bitcast.26), calls=%async_computation.2 | async-start | bytes 524288 | tf_op jit(solution)/shard_map/all_to_all | solution.py:522
  196.7 0.0 all-gather.5.cloned.1.call-done
  196.7 1.6 fold.1._.small
  198.3 4.5 %collective-permute-start.11 = (f32[40,128]{1,0:T(8,128)}, f32[40,128]{1,0:T(8,128)S(1)}, u32[]{:S(2)}, u32[]{:S(2)}) collective-permute-start(f32[40,128]{1,0:T(8,128)} %fold.1._.small), channel_id=1, source_target_pairs={{0,8},{8,0},{1,9},{9,1},{2,10},{10,2},{3,11},{11,3},{4,12},{12,4},... | collective-permute-start | bytes 61448 | tf_op jit(solution)/shard_map/ppermute | solution.py:524
  202.8 0.7 copy-done.2
  203.5 0.8 copy-done.4
  204.4 5.0 %join.1 = (bf16[128,8192]{1,0:T(8,128)(2,1)}, f32[8,128]{1,0:T(8,128)S(1)}) custom-call(s32[2]{0:T(128)S(1)} %copy-done.5, bf16[256,32]{1,0:T(8,128)(2,1)S(1)} %copy-done.4, bf16[32,8192]{1,0:T(8,128)(2,1)S(1)} %copy-done, bf16[128,8192]{1,0:T(8,128)(2,1)S(1)} %copy-done.1, bf16[128,8192]{1,0:T(8,128)(2,1)} %collective-permute-done.10.theirs, ...), custom_call_target="tpu_custom_call" | custom-call | tf_op jit(solution)/shard_map/join/pallas_call | solution.py:382
  209.4 1.4 all-to-all-done.2
  210.7 0.8 finish.1
  (35 shorter events, 0.1 us)
Async XLA Ops:
  7.2 20.0 %slice-start.1 = ((bf16[8192,128]{1,0:T(8,128)(2,1)}), bf16[3072,128]{1,0:T(8,128)(2,1)S(1)}, s32[]{:S(2)}) async-start(bf16[8192,128]{1,0:T(8,128)(2,1)} %own_val.5), calls=%async_computation.6 | async-start | bytes 1572864 | tf_op jit(solution)/shard_map/slice | solution.py:486
  7.2 20.0 %slice-start = ((bf16[8192,128]{1,0:T(8,128)(2,1)}), bf16[3072,128]{1,0:T(8,128)(2,1)S(1)}, s32[]{:S(2)}) async-start(bf16[8192,128]{1,0:T(8,128)(2,1)} %own_key.5), calls=%async_computation.5 | async-start | bytes 1572864 | tf_op jit(solution)/shard_map/slice | solution.py:486
  7.2 20.0 %copy-start.13 = (bf16[32,128]{1,0:T(8,128)(2,1)S(1)}, bf16[32,128]{1,0:T(8,128)(2,1)}, u32[]{:S(2)}) copy-start(bf16[32,128]{1,0:T(8,128)(2,1)} %param.12) | copy-start | bytes 24580
  7.2 90.3 %all-gather.3.cloned.1.call-start = ((), (), s32[]{:S(2)}) async-start(), calls=%async_computation.3 | async-start | bytes 8355840 | tf_op jit(solution)/shard_map/all_gather | solution.py:485
  8.3 14.3 %collective-permute-start.1 = (bf16[320,256]{1,0:T(8,128)(2,1)S(1)}, bf16[320,256]{1,0:T(8,128)(2,1)S(1)}, u32[]{:S(2)}, u32[]{:S(2)}) collective-permute-start(bf16[320,256]{1,0:T(8,128)(2,1)S(1)} %pad_maximum_fusion.3), channel_id=1, source_target_pairs={{0,14},{2,0},{4,2},{6,4},{8,6},{10,8},{12,10},{14,12},{1,15},{3,1}... | collective-permute-start | bytes 491528 | tf_op jit(solution)/shard_map/ppermute | solution.py:474
  14.8 7.8 %collective-permute-start.4 = (bf16[320,256]{1,0:T(8,128)(2,1)S(1)}, bf16[320,256]{1,0:T(8,128)(2,1)S(1)}, u32[]{:S(2)}, u32[]{:S(2)}) collective-permute-start(bf16[320,256]{1,0:T(8,128)(2,1)S(1)} %pad_maximum_fusion.3), channel_id=1, source_target_pairs={{0,2},{2,4},{4,6},{6,8},{8,10},{10,12},{12,14},{14,0},{1,3},{3,5},... | collective-permute-start | bytes 491528 | tf_op jit(solution)/shard_map/ppermute | solution.py:474
  14.8 6.7 %collective-permute-start.2 = (bf16[160,256]{1,0:T(8,128)(2,1)S(1)}, bf16[160,256]{1,0:T(8,128)(2,1)S(1)}, u32[]{:S(2)}, u32[]{:S(2)}) collective-permute-start(bf16[160,256]{1,0:T(8,128)(2,1)S(1)} %get-tuple-element.28), channel_id=1, source_target_pairs={{0,12},{2,14},{4,0},{6,2},{8,4},{10,6},{12,8},{14,10},{1,13},{3,15... | collective-permute-start | bytes 245768 | tf_op jit(solution)/shard_map/ppermute | solution.py:474
  16.8 5.8 %collective-permute-start.3 = (bf16[160,256]{1,0:T(8,128)(2,1)S(1)}, bf16[160,256]{1,0:T(8,128)(2,1)S(1)}, u32[]{:S(2)}, u32[]{:S(2)}) collective-permute-start(bf16[160,256]{1,0:T(8,128)(2,1)S(1)} %get-tuple-element.29), channel_id=1, source_target_pairs={{0,4},{2,6},{4,8},{6,10},{8,12},{10,14},{12,0},{14,2},{1,5},{3,7},... | collective-permute-start | bytes 245768 | tf_op jit(solution)/shard_map/ppermute | solution.py:474
  23.4 48.8 %collective-permute-start = (bf16[128,8192]{1,0:T(8,128)(2,1)}, bf16[128,8192]{1,0:T(8,128)(2,1)}, u32[]{:S(2)}, u32[]{:S(2)}) collective-permute-start(bf16[128,8192]{1,0:T(8,128)(2,1)} %param.8), channel_id=1, source_target_pairs={{0,1},{1,0},{2,3},{3,2},{4,5},{5,4},{6,7},{7,6},{8,9},{9,8},{10,11... | collective-permute-start | bytes 6291464 | tf_op jit(solution)/shard_map/ppermute | solution.py:500
  29.2 37.7 %collective-permute-start.5 = (bf16[3104,256]{1,0:T(8,128)(2,1)}, bf16[3104,256]{1,0:T(8,128)(2,1)S(1)}, u32[]{:S(2)}, u32[]{:S(2)}) collective-permute-start(bf16[3104,256]{1,0:T(8,128)(2,1)} %fusion.5), channel_id=1, source_target_pairs={{0,14},{2,0},{4,2},{6,4},{8,6},{10,8},{12,10},{14,12},{1,15},{3,1}... | collective-permute-start | bytes 4767752 | tf_op jit(solution)/shard_map/ppermute | solution.py:474
  30.4 38.9 %collective-permute-start.7 = (bf16[3104,256]{1,0:T(8,128)(2,1)}, bf16[3104,256]{1,0:T(8,128)(2,1)}, u32[]{:S(2)}, u32[]{:S(2)}) collective-permute-start(bf16[3104,256]{1,0:T(8,128)(2,1)} %fusion.5), channel_id=1, source_target_pairs={{0,2},{2,4},{4,6},{6,8},{8,10},{10,12},{12,14},{14,0},{1,3},{3,5},... | collective-permute-start | bytes 4767752 | tf_op jit(solution)/shard_map/ppermute | solution.py:474
  32.1 40.1 %copy-start.11 = (bf16[128,8192]{1,0:T(8,128)(2,1)S(1)}, bf16[128,8192]{1,0:T(8,128)(2,1)}, u32[]{:S(2)}) copy-start(bf16[128,8192]{1,0:T(8,128)(2,1)} %param.8) | copy-start | bytes 6291460
  34.1 0.8 copy-start.9
  34.1 1.6 copy-start.10
  66.9 8.6 %copy-start.8 = (bf16[3104,256]{1,0:T(8,128)(2,1)}, bf16[3104,256]{1,0:T(8,128)(2,1)S(1)}, u32[]{:S(2)}) copy-start(bf16[3104,256]{1,0:T(8,128)(2,1)S(1)} %collective-permute-done.5.one) | copy-start | bytes 4767748
  68.0 19.3 %collective-permute-start.6 = (bf16[1568,256]{1,0:T(8,128)(2,1)}, bf16[1568,256]{1,0:T(8,128)(2,1)}, u32[]{:S(2)}, u32[]{:S(2)}) collective-permute-start(bf16[1568,256]{1,0:T(8,128)(2,1)} %slice.44), channel_id=1, source_target_pairs={{0,14},{2,0},{4,2},{6,4},{8,6},{10,8},{12,10},{14,12},{1,15},{3,1}... | collective-permute-start | bytes 2408456 | tf_op jit(solution)/shard_map/ppermute | solution.py:474
  71.3 19.5 %collective-permute-start.8 = (bf16[1536,256]{1,0:T(8,128)(2,1)}, bf16[1536,256]{1,0:T(8,128)(2,1)}, u32[]{:S(2)}, u32[]{:S(2)}) collective-permute-start(bf16[1536,256]{1,0:T(8,128)(2,1)} %slice.45), channel_id=1, source_target_pairs={{0,2},{2,4},{4,6},{6,8},{8,10},{10,12},{12,14},{14,0},{1,3},{3,5},... | collective-permute-start | bytes 2359304 | tf_op jit(solution)/shard_map/ppermute | solution.py:474
  72.2 5.2 %copy-start = (bf16[32,8192]{1,0:T(8,128)(2,1)S(1)}, bf16[32,8192]{1,0:T(8,128)(2,1)}, u32[]{:S(2)}) copy-start(bf16[32,8192]{1,0:T(8,128)(2,1)} %factor.1) | copy-start | bytes 1572868
  75.5 2.0 copy-start.6
  106.1 7.3 %copy-start.7 = (bf16[8192,128]{1,0:T(8,128)(2,1)S(1)}, bf16[8192,128]{1,0:T(8,128)(2,1)}, u32[]{:S(2)}) copy-start(bf16[8192,128]{1,0:T(8,128)(2,1)} %own_val.5) | copy-start | bytes 6291460
  106.1 26.5 %all-to-all-start = ((bf16[4,288,384]{2,1,0:T(8,128)(2,1)}), bf16[4,288,384]{2,1,0:T(8,128)(2,1)}, u32[]{:S(2)}, u32[]{:S(2)}) async-start(bf16[4,288,384]{2,1,0:T(8,128)(2,1)} %project.1), calls=%async_computation | async-start | bytes 1769472 | tf_op jit(solution)/shard_map/all_to_all | solution.py:514
  110.7 85.9 %all-gather.5.cloned.1.call-start = ((), (), s32[]{:S(2)}) async-start(), calls=%async_computation.4 | async-start | bytes 2228224 | tf_op jit(solution)/shard_map/all_gather | solution.py:517
  113.4 1.3 copy-start.14
  173.5 29.3 %collective-permute-start.10 = (bf16[128,8192]{1,0:T(8,128)(2,1)}, bf16[128,8192]{1,0:T(8,128)(2,1)}, u32[]{:S(2)}, u32[]{:S(2)}) collective-permute-start(bf16[128,8192]{1,0:T(8,128)(2,1)} %get-tuple-element.21), channel_id=1, source_target_pairs={{0,1},{1,0},{2,3},{3,2},{4,5},{5,4},{6,7},{7,6},{8,9},{9,8},{10,11... | collective-permute-start | bytes 6291464 | tf_op jit(solution)/shard_map/ppermute | solution.py:520
  175.3 27.5 %copy-start.1 = (bf16[128,8192]{1,0:T(8,128)(2,1)S(1)}, bf16[128,8192]{1,0:T(8,128)(2,1)}, u32[]{:S(2)}) copy-start(bf16[128,8192]{1,0:T(8,128)(2,1)} %get-tuple-element.20.mine) | copy-start | bytes 6291460
  175.3 27.5 %copy-start.5 = (s32[2]{0:T(128)S(1)}, s32[2]{0:T(128)}, u32[]{:S(2)}) copy-start(s32[2]{0:T(128)} %pad_add_fusion.place) | copy-start | bytes 28
  175.3 4.2 %collective-permute-start.9 = (f32[256,32]{1,0:T(8,128)}, f32[256,32]{1,0:T(8,128)S(1)}, u32[]{:S(2)}, u32[]{:S(2)}) collective-permute-start(f32[256,32]{1,0:T(8,128)} %get-tuple-element.18.part), channel_id=1, source_target_pairs={{0,1},{1,0},{2,3},{3,2},{4,5},{5,4},{6,7},{7,6},{8,9},{9,8},{10,11... | collective-permute-start | bytes 98312 | tf_op jit(solution)/shard_map/ppermute | solution.py:519
  179.5 0.7 copy-start.12
  184.7 26.1 %all-to-all-start.2 = ((bf16[128,8,128]{2,1,0:T(8,128)(2,1)}), bf16[128,8,128]{2,1,0:T(8,128)(2,1)S(1)}, u32[]{:S(2)}, u32[]{:S(2)}) async-start(bf16[128,8,128]{2,1,0:T(8,128)(2,1)} %bitcast.26), calls=%async_computation.2 | async-start | bytes 524288 | tf_op jit(solution)/shard_map/all_to_all | solution.py:522
  198.3 12.4 %collective-permute-start.11 = (f32[40,128]{1,0:T(8,128)}, f32[40,128]{1,0:T(8,128)S(1)}, u32[]{:S(2)}, u32[]{:S(2)}) collective-permute-start(f32[40,128]{1,0:T(8,128)} %fold.1._.small), channel_id=1, source_target_pairs={{0,8},{8,0},{1,9},{9,1},{2,10},{10,2},{3,11},{11,3},{4,12},{12,4},... | collective-permute-start | bytes 61448 | tf_op jit(solution)/shard_map/ppermute | solution.py:524
  202.8 0.8 copy-start.2
  203.5 0.8 copy-start.4
  204.4 6.3 %copy-start.3 = (f32[40,128]{1,0:T(8,128)S(1)}, f32[40,128]{1,0:T(8,128)}, u32[]{:S(2)}) copy-start(f32[40,128]{1,0:T(8,128)} %fold.1._.small) | copy-start | bytes 61444
Sparse Core Ops, SparseCore 0:
  23.6 73.8 all-gather.2
  144.7 49.2 all-gather.4

commit v3 on v2

--- a/solution.py
+++ b/solution.py
@@ -211,8 +211,9 @@
     )(place, pair, w_key, w_val, far, so_far, down, ups, cos, sin)
 
 
-def attend_kernel(query, grad, rows, col_scale, norms, cos, sin, grads, small, keys, vals, dkey, dval):
+def attend_kernel(query, grad, rows, col_scale, norms, cos_far, sin_far, grads, small, keys, vals, dkey, dval, cos, sin, sems):
     step = pl.program_id(0)
+    tables = [pltpu.make_async_copy(cos_far, cos, sems.at[0]), pltpu.make_async_copy(sin_far, sin, sems.at[1])]
 
     @pl.when(step == 0)
     def _():
@@ -222,6 +223,7 @@
             vals[here, :] = (rows[i, :PAIR, 2 * HD :].astype(F32) * col_scale[...]).astype(BF)
         dkey[...] = jnp.zeros_like(dkey)
         dval[...] = jnp.zeros_like(dval)
+        start_all(tables)
 
     for block in range(SEQ // QB):
         stop = (block + 1) * QB
@@ -257,6 +259,7 @@
 
     @pl.when(step == pl.num_programs(0) - 1)
     def _():
+        wait_all(tables)
         dk = dkey[...] * INV_SQRT
         dk = dk * cos[...] - pltpu.roll(dk, HD // 2, 1) * sin[...]
         dv = dval[...]
@@ -286,8 +289,8 @@
             whole((4, PAIR + 32, 3 * HD)),
             whole((1, HD)),
             whole((1, HD)),
-            whole((SEQ, HD)),
-            whole((SEQ, HD)),
+            any_ref(),
+            any_ref(),
         ],
         out_specs=[whole((SEQ, 2 * HD)), whole((SMALL, HD))],
         out_shape=[jax.ShapeDtypeStruct((SEQ, 2 * HD), BF), jax.ShapeDtypeStruct((SMALL, HD), F32)],
@@ -296,6 +299,9 @@
             pltpu.VMEM((SEQ, HD), BF),
             pltpu.VMEM((SEQ, HD), F32),
             pltpu.VMEM((SEQ, HD), F32),
+            pltpu.VMEM((SEQ, HD), F32),
+            pltpu.VMEM((SEQ, HD), F32),
+            pltpu.SemaphoreType.DMA((2,)),
         ],
         compiler_params=params(60),
         cost_estimate=cost(5 * 2 * GROUP * SEQ * SEQ * HD, 6 * MIB, GROUP * SEQ * SEQ),

time: 219 us -> 219 us (level)
  no operation moved by 1% of the time
where the time goes in v3:
time: 219 us; the launch traced here: 218 us
  waiting for transfers between devices  69.5 us (32%)
  Pallas kernels  49.2 us (22%)
  starting transfers between devices  38.6 us (18%)
  blocking collectives  18 us (8%)
  other arithmetic  14.5 us (7%)
  between operations  14.2 us (6%)
  local copies, waits for them, and re-layouts  11.4 us (5%)
  matrix products  2.65 us (1%)
    ppermute x8, waiting for transfers between devices, along_z(): lax.ppermute(value, ('zh', 'zl'), [(i, (i + shift) % 8) for i in range(8)])  46.4 us
    all_to_all x1, blocking collectives, shards(): lax.all_to_all(grads.reshape(4, PAIR, 2 * HD), 'zl', 0, 0, tiled=True)  18 us
    all_to_all x1, waiting for transfers between devices, shards(): rows = lax.all_to_all(rows, 'zl', 0, 0, tiled=True)  17.3 us
    ppermute x8, starting transfers between devices, along_z(): lax.ppermute(value, ('zh', 'zl'), [(i, (i + shift) % 8) for i in range(8)])  12.7 us
    all_to_all x1, starting transfers between devices, shards(): pieces = lax.all_to_all(pieces, DP + ('zl',), 0, 0, tiled=True)  12 us
    pallas_call x1, Pallas kernels, attend(): pl.pallas_call(attend_kernel, grid=(GROUP // HEADS,), in_specs=[pl.BlockS...  11.7 us
    pallas_call x1, Pallas kernels, back(): pl.pallas_call(back_kernel, in_specs=[smem(), in_vmem(), in_vmem()] + [an...  10.9 us
    pallas_call x1, Pallas kernels, project(): pl.pallas_call(project_kernel, in_specs=[smem(), any_ref(), any_ref(), an...  8.54 us
  transfers between devices with their start and end apart: 16, of which 9 were waited for; matrix products, arithmetic and copies ran while one was open for 10% of the time, Pallas kernels for 13%

profile of v3, /device:TPU:1, one launch (start us, length us, event | category | flops | bytes accessed | tf_op | source)
XLA Modules:
  0.0 218.1 jit_solution(10579685907707312523)
XLA Ops:
  7.2 0.0 slice-start.1
  7.2 0.0 slice-start
  7.2 0.0 all-gather.3.cloned.1.call-start
  7.3 1.0 constant_dynamic-slice_fusion.1
  8.3 6.5 %collective-permute-start.1 = (bf16[320,256]{1,0:T(8,128)(2,1)S(1)}, bf16[320,256]{1,0:T(8,128)(2,1)S(1)}, u32[]{:S(2)}, u32[]{:S(2)}) collective-permute-start(bf16[320,256]{1,0:T(8,128)(2,1)S(1)} %pad_maximum_fusion.3), channel_id=1, source_target_pairs={{0,14},{2,0},{4,2},{6,4},{8,6},{10,8},{12,10},{14,12},{1,15},{3,1}... | collective-permute-start | bytes 491528 | tf_op jit(solution)/shard_map/ppermute | solution.py:480
  14.8 0.0 collective-permute-start.4
  14.8 2.0 collective-permute-start.2
  16.8 0.5 collective-permute-start.3
  17.3 4.3 %collective-permute-done.2 = bf16[160,256]{1,0:T(8,128)(2,1)S(1)} collective-permute-done((bf16[160,256]{1,0:T(8,128)(2,1)S(1)}, bf16[160,256]{1,0:T(8,128)(2,1)S(1)}, u32[]{:S(2)}, u32[]{:S(2)}) %collective-permute-start.2) | collective-permute-done | bytes 81952 | tf_op jit(solution)/shard_map/ppermute | solution.py:480
  21.6 1.0 collective-permute-done.3
  22.6 0.8 pad_maximum_fusion.2
  23.4 0.0 all-gather.3.cloned.1.call-update
  23.4 2.5 %collective-permute-start = (bf16[128,8192]{1,0:T(8,128)(2,1)}, bf16[128,8192]{1,0:T(8,128)(2,1)}, u32[]{:S(2)}, u32[]{:S(2)}) collective-permute-start(bf16[128,8192]{1,0:T(8,128)(2,1)} %param.8), channel_id=1, source_target_pairs={{0,1},{1,0},{2,3},{3,2},{4,5},{5,4},{6,7},{7,6},{8,9},{9,8},{10,11... | collective-permute-start | bytes 6291464 | tf_op jit(solution)/shard_map/ppermute | solution.py:506
  26.0 1.2 fusion.13
  27.2 2.1 fusion.5
  29.2 1.1 collective-permute-start.5
  30.4 1.2 collective-permute-start.7
  31.5 0.6 pad_add_fusion.place
  32.1 2.0 fusion.6
  34.1 0.8 copy-done.9
  34.9 0.8 fusion.9
  35.7 31.2 %collective-permute-done.5.one = bf16[3104,256]{1,0:T(8,128)(2,1)S(1)} collective-permute-done((bf16[3104,256]{1,0:T(8,128)(2,1)}, bf16[3104,256]{1,0:T(8,128)(2,1)S(1)}, u32[]{:S(2)}, u32[]{:S(2)}) %collective-permute-start.5) | collective-permute-done | bytes 1589280 | tf_op jit(solution)/shard_map/ppermute | solution.py:480
  66.9 1.1 slice.44
  68.0 1.2 collective-permute-start.6
  69.2 2.1 slice.45
  71.3 0.2 collective-permute-start.8
  71.5 0.7 slice_bitcast_fusion
  72.3 3.2 %maximum_select_fusion.pair = bf16[256,8192]{1,0:T(8,128)(2,1)S(1)} fusion(bf16[128,8192]{1,0:T(8,128)(2,1)} %collective-permute-done, bf16[128,8192]{1,0:T(8,128)(2,1)S(1)} %copy-done.11, pred[]{:T(512)S(6)} %eq.3), kind=kLoop, calls=%fused_computation.3 | loop fusion | flops 18874368 | bytes 8388609 | tf_op jit(solution)/shard_map/jit(_where)/select_n | solution.py:507
  75.5 2.0 copy-done.6
  77.5 1.4 convolution_convert_fusion
  78.8 0.7 copy.13.down
  79.6 7.7 %collective-permute-done.6.two_a = bf16[1568,256]{1,0:T(8,128)(2,1)} collective-permute-done((bf16[1568,256]{1,0:T(8,128)(2,1)}, bf16[1568,256]{1,0:T(8,128)(2,1)}, u32[]{:S(2)}, u32[]{:S(2)}) %collective-permute-start.6) | collective-permute-done | bytes 802848 | tf_op jit(solution)/shard_map/ppermute | solution.py:480
  87.3 0.7 slice_bitcast_fusion.1
  88.0 0.6 pad_maximum_fusion.4.ups
  88.6 2.2 %collective-permute-done.8.two_b = bf16[1536,256]{1,0:T(8,128)(2,1)} collective-permute-done((bf16[1536,256]{1,0:T(8,128)(2,1)}, bf16[1536,256]{1,0:T(8,128)(2,1)}, u32[]{:S(2)}, u32[]{:S(2)}) %collective-permute-start.8) | collective-permute-done | bytes 786464 | tf_op jit(solution)/shard_map/ppermute | solution.py:480
  90.8 6.1 %project_line.1.so_far = f32[256,1024]{1,0:T(8,128)} custom-call(bf16[256,8192]{1,0:T(8,128)(2,1)} %copy-done.6, bf16[8192,128]{1,0:T(8,128)(2,1)} %own_key.5, bf16[8192,128]{1,0:T(8,128)(2,1)} %own_val.5, bf16[3104,256]{1,0:T(8,128)(2,1)} %copy-done.8, bf16[1568,256]{1,0:T(8,128)(2,1)} %collective-permute-done.6.two_a, ...), custom_call_target="tpu_custom_call" | custom-call | flops 1610612736 | bytes 8388608 | tf_op jit(solution)/shard_map/project_line/pallas_call | solution.py:143
  96.9 0.6 all-gather.3.cloned.1.call-done.far
  97.5 8.5 %project.1 = bf16[4,288,384]{2,1,0:T(8,128)(2,1)} custom-call(s32[2]{0:T(128)} %pad_add_fusion.place, bf16[256,8192]{1,0:T(8,128)(2,1)} %copy-done.6, bf16[8192,128]{1,0:T(8,128)(2,1)} %own_key.5, bf16[8192,128]{1,0:T(8,128)(2,1)} %own_val.5, bf16[5120,768]{1,0:T(8,128)(2,1)} %all-gather.3.cloned.1.call-done.far, f32[256,1024]{1,0:T(8,128)} %project_line.1.so_far, ...), custom_call_target="tpu_custom_call" | custom-call | flops 2684354560 | bytes 14680064 | tf_op jit(solution)/shard_map/project/pallas_call | solution.py:186
  106.1 0.0 copy-start.7
  106.1 4.7 %all-to-all-start = ((bf16[4,288,384]{2,1,0:T(8,128)(2,1)}), bf16[4,288,384]{2,1,0:T(8,128)(2,1)}, u32[]{:S(2)}, u32[]{:S(2)}) async-start(bf16[4,288,384]{2,1,0:T(8,128)(2,1)} %project.1), calls=%async_computation | async-start | bytes 1769472 | tf_op jit(solution)/shard_map/all_to_all | solution.py:520
  110.7 0.0 all-gather.5.cloned.1.call-start
  110.7 2.7 %pad_maximum_fusion = (f32[1024,128]{1,0:T(8,128)}, f32[1024,128]{1,0:T(8,128)}) fusion(f32[1024,64]{1,0:T(8,128)} %copy-done.10, f32[1024,64]{1,0:T(8,128)S(1)} %get-tuple-element.32, f32[1024,64]{1,0:T(8,128)} %copy-done.9), kind=kLoop, calls=%fused_computation.14 | loop fusion | flops 262144 | bytes 1835008 | tf_op jit(solution)/shard_map/concatenate | solution.py:39
  113.4 1.3 fusion.3
  114.7 0.5 sqrt_bitcast_fusion
  115.2 17.3 %all-to-all-done.rows = bf16[4,288,384]{2,1,0:T(8,128)(2,1)} async-done(((bf16[4,288,384]{2,1,0:T(8,128)(2,1)}), bf16[4,288,384]{2,1,0:T(8,128)(2,1)}, u32[]{:S(2)}, u32[]{:S(2)}) %all-to-all-start) | async-done | bytes 884768 | tf_op jit(solution)/shard_map/all_to_all | solution.py:520
  132.6 11.7 %attend.1 = (bf16[1024,256]{1,0:T(8,128)(2,1)}, f32[256,128]{1,0:T(8,128)}) custom-call(bf16[1024,512]{1,0:T(8,128)(2,1)} %query.1, bf16[1024,512]{1,0:T(8,128)(2,1)} %grad.1, bf16[4,288,384]{2,1,0:T(8,128)(2,1)} %all-to-all-done.rows, f32[1,128]{1,0:T(1,128)} %get-tuple-element.31.col_scale, f32[1,128]{1,0:T(1,128)} %get-tuple-element.30.norms, ...), custom_call_target="tpu_custom_call" | custom-call | flops 5368709120 | bytes 6291456 | tf_op jit(solution)/shard_map/attend/pallas_call | solution.py:283
  144.3 0.0 all-gather.5.cloned.1.call-update
  144.3 18.0 %all_to_all.21.grads = bf16[4,256,256]{2,1,0:T(8,128)(2,1)} all-to-all(bf16[4,256,256]{2,1,0:T(8,128)(2,1)} %bitcast.25), channel_id=1, replica_groups=mesh['x'=4,'y'=4,'zh'=2,'zl'=4,'core'=2] {'zl'}, dimensions={0} | all-to-all | bytes 1048576 | tf_op jit(solution)/shard_map/all_to_all | solution.py:522
  162.3 10.9 %back.1 = (bf16[128,8192]{1,0:T(8,128)(2,1)}, bf16[128,8192]{1,0:T(8,128)(2,1)}, f32[256,32]{1,0:T(8,128)}) custom-call(s32[2]{0:T(128)} %pad_add_fusion.place, bf16[4,256,256]{2,1,0:T(8,128)(2,1)} %all_to_all.21.grads, bf16[4,32,128]{2,1,0:T(8,128)(2,1)} %pad_maximum_fusion.4.ups, bf16[8192,128]{1,0:T(8,128)(2,1)} %own_key.5, bf16[8192,128]{1,0:T(8,128)(2,1)} %own_val.5, ...), custom_call_target="tpu_custom_call" | custom-call | tf_op jit(solution)/shard_map/back/pallas_call | solution.py:349
  173.2 1.8 collective-permute-start.10
  175.0 0.4 collective-permute-start.9
  175.4 3.8 %collective-permute-done.9.got = f32[256,32]{1,0:T(8,128)S(1)} collective-permute-done((f32[256,32]{1,0:T(8,128)}, f32[256,32]{1,0:T(8,128)S(1)}, u32[]{:S(2)}, u32[]{:S(2)}) %collective-permute-start.9) | collective-permute-done | bytes 32800 | tf_op jit(solution)/shard_map/ppermute | solution.py:525
  179.2 0.6 copy-done.12
  179.8 4.5 %down_part.1 = (bf16[1024,128]{1,0:T(8,128)(2,1)}, bf16[256,32]{1,0:T(8,128)(2,1)}) custom-call(s32[2]{0:T(128)} %pad_add_fusion.place, f32[256,32]{1,0:T(8,128)} %get-tuple-element.18.part, f32[256,32]{1,0:T(8,128)} %copy-done.12, bf16[256,8192]{1,0:T(8,128)(2,1)} %copy-done.6), custom_call_target="tpu_custom_call" | custom-call | flops 134217728 | bytes 5242880 | tf_op jit(solution)/shard_map/down_part/pallas_call | solution.py:425
  184.4 12.0 %all-to-all-start.2 = ((bf16[128,8,128]{2,1,0:T(8,128)(2,1)}), bf16[128,8,128]{2,1,0:T(8,128)(2,1)S(1)}, u32[]{:S(2)}, u32[]{:S(2)}) async-start(bf16[128,8,128]{2,1,0:T(8,128)(2,1)} %bitcast.26), calls=%async_computation.2 | async-start | bytes 524288 | tf_op jit(solution)/shard_map/all_to_all | solution.py:528
  196.4 0.0 all-gather.5.cloned.1.call-done
  196.4 1.6 fold.1._.small
  198.0 4.5 %collective-permute-start.11 = (f32[40,128]{1,0:T(8,128)}, f32[40,128]{1,0:T(8,128)S(1)}, u32[]{:S(2)}, u32[]{:S(2)}) collective-permute-start(f32[40,128]{1,0:T(8,128)} %fold.1._.small), channel_id=1, source_target_pairs={{0,8},{8,0},{1,9},{9,1},{2,10},{10,2},{3,11},{11,3},{4,12},{12,4},... | collective-permute-start | bytes 61448 | tf_op jit(solution)/shard_map/ppermute | solution.py:530
  202.5 0.7 copy-done.2
  203.2 0.8 copy-done.4
  204.1 5.0 %join.1 = (bf16[128,8192]{1,0:T(8,128)(2,1)}, f32[8,128]{1,0:T(8,128)S(1)}) custom-call(s32[2]{0:T(128)S(1)} %copy-done.5, bf16[256,32]{1,0:T(8,128)(2,1)S(1)} %copy-done.4, bf16[32,8192]{1,0:T(8,128)(2,1)S(1)} %copy-done, bf16[128,8192]{1,0:T(8,128)(2,1)S(1)} %copy-done.1, bf16[128,8192]{1,0:T(8,128)(2,1)} %collective-permute-done.10.theirs, ...), custom_call_target="tpu_custom_call" | custom-call | tf_op jit(solution)/shard_map/join/pallas_call | solution.py:388
  209.1 1.4 all-to-all-done.2
  210.4 0.0 collective-permute-done.11.other
  210.4 0.8 finish.1
  (35 shorter events, 0.1 us)
Async XLA Ops:
  7.2 20.0 %slice-start.1 = ((bf16[8192,128]{1,0:T(8,128)(2,1)}), bf16[3072,128]{1,0:T(8,128)(2,1)S(1)}, s32[]{:S(2)}) async-start(bf16[8192,128]{1,0:T(8,128)(2,1)} %own_val.5), calls=%async_computation.6 | async-start | bytes 1572864 | tf_op jit(solution)/shard_map/slice | solution.py:492
  7.2 20.0 %slice-start = ((bf16[8192,128]{1,0:T(8,128)(2,1)}), bf16[3072,128]{1,0:T(8,128)(2,1)S(1)}, s32[]{:S(2)}) async-start(bf16[8192,128]{1,0:T(8,128)(2,1)} %own_key.5), calls=%async_computation.5 | async-start | bytes 1572864 | tf_op jit(solution)/shard_map/slice | solution.py:492
  7.2 20.0 %copy-start.13 = (bf16[32,128]{1,0:T(8,128)(2,1)S(1)}, bf16[32,128]{1,0:T(8,128)(2,1)}, u32[]{:S(2)}) copy-start(bf16[32,128]{1,0:T(8,128)(2,1)} %param.12) | copy-start | bytes 24580
  7.2 90.3 %all-gather.3.cloned.1.call-start = ((), (), s32[]{:S(2)}) async-start(), calls=%async_computation.3 | async-start | bytes 8355840 | tf_op jit(solution)/shard_map/all_gather | solution.py:491
  8.3 14.3 %collective-permute-start.1 = (bf16[320,256]{1,0:T(8,128)(2,1)S(1)}, bf16[320,256]{1,0:T(8,128)(2,1)S(1)}, u32[]{:S(2)}, u32[]{:S(2)}) collective-permute-start(bf16[320,256]{1,0:T(8,128)(2,1)S(1)} %pad_maximum_fusion.3), channel_id=1, source_target_pairs={{0,14},{2,0},{4,2},{6,4},{8,6},{10,8},{12,10},{14,12},{1,15},{3,1}... | collective-permute-start | bytes 491528 | tf_op jit(solution)/shard_map/ppermute | solution.py:480
  14.8 7.8 %collective-permute-start.4 = (bf16[320,256]{1,0:T(8,128)(2,1)S(1)}, bf16[320,256]{1,0:T(8,128)(2,1)S(1)}, u32[]{:S(2)}, u32[]{:S(2)}) collective-permute-start(bf16[320,256]{1,0:T(8,128)(2,1)S(1)} %pad_maximum_fusion.3), channel_id=1, source_target_pairs={{0,2},{2,4},{4,6},{6,8},{8,10},{10,12},{12,14},{14,0},{1,3},{3,5},... | collective-permute-start | bytes 491528 | tf_op jit(solution)/shard_map/ppermute | solution.py:480
  14.8 6.7 %collective-permute-start.2 = (bf16[160,256]{1,0:T(8,128)(2,1)S(1)}, bf16[160,256]{1,0:T(8,128)(2,1)S(1)}, u32[]{:S(2)}, u32[]{:S(2)}) collective-permute-start(bf16[160,256]{1,0:T(8,128)(2,1)S(1)} %get-tuple-element.28), channel_id=1, source_target_pairs={{0,12},{2,14},{4,0},{6,2},{8,4},{10,6},{12,8},{14,10},{1,13},{3,15... | collective-permute-start | bytes 245768 | tf_op jit(solution)/shard_map/ppermute | solution.py:480
  16.8 5.8 %collective-permute-start.3 = (bf16[160,256]{1,0:T(8,128)(2,1)S(1)}, bf16[160,256]{1,0:T(8,128)(2,1)S(1)}, u32[]{:S(2)}, u32[]{:S(2)}) collective-permute-start(bf16[160,256]{1,0:T(8,128)(2,1)S(1)} %get-tuple-element.29), channel_id=1, source_target_pairs={{0,4},{2,6},{4,8},{6,10},{8,12},{10,14},{12,0},{14,2},{1,5},{3,7},... | collective-permute-start | bytes 245768 | tf_op jit(solution)/shard_map/ppermute | solution.py:480
  23.4 48.8 %collective-permute-start = (bf16[128,8192]{1,0:T(8,128)(2,1)}, bf16[128,8192]{1,0:T(8,128)(2,1)}, u32[]{:S(2)}, u32[]{:S(2)}) collective-permute-start(bf16[128,8192]{1,0:T(8,128)(2,1)} %param.8), channel_id=1, source_target_pairs={{0,1},{1,0},{2,3},{3,2},{4,5},{5,4},{6,7},{7,6},{8,9},{9,8},{10,11... | collective-permute-start | bytes 6291464 | tf_op jit(solution)/shard_map/ppermute | solution.py:506
  29.2 37.7 %collective-permute-start.5 = (bf16[3104,256]{1,0:T(8,128)(2,1)}, bf16[3104,256]{1,0:T(8,128)(2,1)S(1)}, u32[]{:S(2)}, u32[]{:S(2)}) collective-permute-start(bf16[3104,256]{1,0:T(8,128)(2,1)} %fusion.5), channel_id=1, source_target_pairs={{0,14},{2,0},{4,2},{6,4},{8,6},{10,8},{12,10},{14,12},{1,15},{3,1}... | collective-permute-start | bytes 4767752 | tf_op jit(solution)/shard_map/ppermute | solution.py:480
  30.4 38.9 %collective-permute-start.7 = (bf16[3104,256]{1,0:T(8,128)(2,1)}, bf16[3104,256]{1,0:T(8,128)(2,1)}, u32[]{:S(2)}, u32[]{:S(2)}) collective-permute-start(bf16[3104,256]{1,0:T(8,128)(2,1)} %fusion.5), channel_id=1, source_target_pairs={{0,2},{2,4},{4,6},{6,8},{8,10},{10,12},{12,14},{14,0},{1,3},{3,5},... | collective-permute-start | bytes 4767752 | tf_op jit(solution)/shard_map/ppermute | solution.py:480
  32.1 40.1 %copy-start.11 = (bf16[128,8192]{1,0:T(8,128)(2,1)S(1)}, bf16[128,8192]{1,0:T(8,128)(2,1)}, u32[]{:S(2)}) copy-start(bf16[128,8192]{1,0:T(8,128)(2,1)} %param.8) | copy-start | bytes 6291460
  34.1 0.8 copy-start.9
  34.1 1.6 copy-start.10
  66.9 8.6 %copy-start.8 = (bf16[3104,256]{1,0:T(8,128)(2,1)}, bf16[3104,256]{1,0:T(8,128)(2,1)S(1)}, u32[]{:S(2)}) copy-start(bf16[3104,256]{1,0:T(8,128)(2,1)S(1)} %collective-permute-done.5.one) | copy-start | bytes 4767748
  68.0 19.3 %collective-permute-start.6 = (bf16[1568,256]{1,0:T(8,128)(2,1)}, bf16[1568,256]{1,0:T(8,128)(2,1)}, u32[]{:S(2)}, u32[]{:S(2)}) collective-permute-start(bf16[1568,256]{1,0:T(8,128)(2,1)} %slice.44), channel_id=1, source_target_pairs={{0,14},{2,0},{4,2},{6,4},{8,6},{10,8},{12,10},{14,12},{1,15},{3,1}... | collective-permute-start | bytes 2408456 | tf_op jit(solution)/shard_map/ppermute | solution.py:480
  71.3 19.5 %collective-permute-start.8 = (bf16[1536,256]{1,0:T(8,128)(2,1)}, bf16[1536,256]{1,0:T(8,128)(2,1)}, u32[]{:S(2)}, u32[]{:S(2)}) collective-permute-start(bf16[1536,256]{1,0:T(8,128)(2,1)} %slice.45), channel_id=1, source_target_pairs={{0,2},{2,4},{4,6},{6,8},{8,10},{10,12},{12,14},{14,0},{1,3},{3,5},... | collective-permute-start | bytes 2359304 | tf_op jit(solution)/shard_map/ppermute | solution.py:480
  72.2 5.2 %copy-start = (bf16[32,8192]{1,0:T(8,128)(2,1)S(1)}, bf16[32,8192]{1,0:T(8,128)(2,1)}, u32[]{:S(2)}) copy-start(bf16[32,8192]{1,0:T(8,128)(2,1)} %factor.1) | copy-start | bytes 1572868
  75.5 2.0 copy-start.6
  106.1 7.3 %copy-start.7 = (bf16[8192,128]{1,0:T(8,128)(2,1)S(1)}, bf16[8192,128]{1,0:T(8,128)(2,1)}, u32[]{:S(2)}) copy-start(bf16[8192,128]{1,0:T(8,128)(2,1)} %own_val.5) | copy-start | bytes 6291460
  106.1 26.5 %all-to-all-start = ((bf16[4,288,384]{2,1,0:T(8,128)(2,1)}), bf16[4,288,384]{2,1,0:T(8,128)(2,1)}, u32[]{:S(2)}, u32[]{:S(2)}) async-start(bf16[4,288,384]{2,1,0:T(8,128)(2,1)} %project.1), calls=%async_computation | async-start | bytes 1769472 | tf_op jit(solution)/shard_map/all_to_all | solution.py:520
  110.7 85.6 %all-gather.5.cloned.1.call-start = ((), (), s32[]{:S(2)}) async-start(), calls=%async_computation.4 | async-start | bytes 2228224 | tf_op jit(solution)/shard_map/all_gather | solution.py:523
  113.4 1.3 copy-start.14
  173.2 29.3 %collective-permute-start.10 = (bf16[128,8192]{1,0:T(8,128)(2,1)}, bf16[128,8192]{1,0:T(8,128)(2,1)}, u32[]{:S(2)}, u32[]{:S(2)}) collective-permute-start(bf16[128,8192]{1,0:T(8,128)(2,1)} %get-tuple-element.21), channel_id=1, source_target_pairs={{0,1},{1,0},{2,3},{3,2},{4,5},{5,4},{6,7},{7,6},{8,9},{9,8},{10,11... | collective-permute-start | bytes 6291464 | tf_op jit(solution)/shard_map/ppermute | solution.py:526
  175.0 27.5 %copy-start.1 = (bf16[128,8192]{1,0:T(8,128)(2,1)S(1)}, bf16[128,8192]{1,0:T(8,128)(2,1)}, u32[]{:S(2)}) copy-start(bf16[128,8192]{1,0:T(8,128)(2,1)} %get-tuple-element.20.mine) | copy-start | bytes 6291460
  175.0 27.5 %copy-start.5 = (s32[2]{0:T(128)S(1)}, s32[2]{0:T(128)}, u32[]{:S(2)}) copy-start(s32[2]{0:T(128)} %pad_add_fusion.place) | copy-start | bytes 28
  175.0 4.2 %collective-permute-start.9 = (f32[256,32]{1,0:T(8,128)}, f32[256,32]{1,0:T(8,128)S(1)}, u32[]{:S(2)}, u32[]{:S(2)}) collective-permute-start(f32[256,32]{1,0:T(8,128)} %get-tuple-element.18.part), channel_id=1, source_target_pairs={{0,1},{1,0},{2,3},{3,2},{4,5},{5,4},{6,7},{7,6},{8,9},{9,8},{10,11... | collective-permute-start | bytes 98312 | tf_op jit(solution)/shard_map/ppermute | solution.py:525
  179.2 0.7 copy-start.12
  184.4 26.1 %all-to-all-start.2 = ((bf16[128,8,128]{2,1,0:T(8,128)(2,1)}), bf16[128,8,128]{2,1,0:T(8,128)(2,1)S(1)}, u32[]{:S(2)}, u32[]{:S(2)}) async-start(bf16[128,8,128]{2,1,0:T(8,128)(2,1)} %bitcast.26), calls=%async_computation.2 | async-start | bytes 524288 | tf_op jit(solution)/shard_map/all_to_all | solution.py:528
  198.0 12.4 %collective-permute-start.11 = (f32[40,128]{1,0:T(8,128)}, f32[40,128]{1,0:T(8,128)S(1)}, u32[]{:S(2)}, u32[]{:S(2)}) collective-permute-start(f32[40,128]{1,0:T(8,128)} %fold.1._.small), channel_id=1, source_target_pairs={{0,8},{8,0},{1,9},{9,1},{2,10},{10,2},{3,11},{11,3},{4,12},{12,4},... | collective-permute-start | bytes 61448 | tf_op jit(solution)/shard_map/ppermute | solution.py:530
  202.5 0.8 copy-start.2
  203.2 0.8 copy-start.4
  204.1 6.3 %copy-start.3 = (f32[40,128]{1,0:T(8,128)S(1)}, f32[40,128]{1,0:T(8,128)}, u32[]{:S(2)}) copy-start(f32[40,128]{1,0:T(8,128)} %fold.1._.small) | copy-start | bytes 61444
Sparse Core Ops, SparseCore 0:
  23.6 73.8 all-gather.2
  144.4 49.2 all-gather.4
